TPU v7x, 32 devices: a whole 2x2x4 slice. The times are simulated.
32 devices in a mesh: dp: 8 (over z, y), section: 4 (over x, core).
Axes of the slice: x: 2, y: 2, z: 4, core: 2. Of those that a mesh axis runs over, the one named last changes fastest.
Arguments:
- encoder_in: bfloat16 [16, 512, 768], P('dp'), may hold values from -6 to 6
- decoder_in: bfloat16 [16, 96, 768], P('dp'), may hold values from -6 to 6
- lengths: int32 [16, 3], P('dp'), may hold values from 64 to 384, as said below
- query_map: int32 [16, 3], P('dp'), may hold values from 0 to 2, as said below
- attn_query: bfloat16 [3, 768, 768], P(None, 'section'), may hold values from -0.02734375 to 0.02734375
- attn_keyval: bfloat16 [6, 768, 768], P(None, 'section'), may hold values from -0.21875 to 0.21875
- attn_output: bfloat16 [3, 768, 768], P(None, 'section'), may hold values from -0.875 to 0.875
- feed_in: bfloat16 [2, 3072, 768], P(None, 'section'), may hold values from -0.21875 to 0.21875
- feed_out: bfloat16 [2, 3072, 768], P(None, 'section'), may hold values from -0.109375 to 0.109375
- norm_gains: float32 [5, 768], replicated, may hold values from 0.5 to 1.5
- position_bias: float32 [2, 32, 12], replicated, may hold values from -4 to 4
- cotangent: bfloat16 [16, 96, 768], P('dp'), may hold values from -6 to 6
Outputs:
- decoder_out: bfloat16 [16, 96, 768], P('dp', 'section')
- encoder_in_grad: bfloat16 [16, 512, 768], P('dp', 'section')
- decoder_in_grad: bfloat16 [16, 96, 768], P('dp', 'section')
- attn_query_grad: float32 [3, 768, 768], P(None, 'section')
- attn_keyval_grad: float32 [6, 768, 768], P(None, 'section')
- attn_output_grad: float32 [3, 768, 768], P(None, 'section')
- feed_in_grad: float32 [2, 3072, 768], P(None, 'section')
- feed_out_grad: float32 [2, 3072, 768], P(None, 'section')
- norm_gains_grad: float32 [5, 768], replicated
- position_bias_grad: float32 [2, 32, 12], replicated
Inputs may be any that keep to these rules, and one draw needn't show every extreme that they name: In every buffer the 3 lengths sum to 512, and the longest is exactly 384. `query_map`: in every buffer each of the 3 queries owns at least one passage.
All inputs are finite; a program needn't handle non-finite values.
Results may differ from a plain program's by a relative error of at most 0.028.
Values may be sent and summed in bfloat16 or wider, within the bound.
No kernel may reach another device: no remote copies, remote signals or barrier semaphores. Data moves between devices by JAX's collectives and lax.ppermute only.
A program may use at most 640 MiB of HBM per device.

v0:
```python
import functools

import jax
import jax.numpy as jnp
import numpy as np
from jax import lax
from jax.experimental import pallas as pl
from jax.experimental.pallas import tpu as pltpu
from jax.sharding import PartitionSpec as P

D = 768
HEADS = 12
HD = 64
PAIRS = HEADS // 2
NB = 32
BUF = 512
BIG = 384
SMALL = 64
REST = BUF - BIG
QPB = 3
TGT = 32
DEC = QPB * TGT
WIDE = 512
epsilon = 1e-06
masked_score = -1e30
enc_edges = (12, 16, 23, 32, 46, 64, 91)
dec_edges = (19, 21, 24, 27, 31)
bf16 = jnp.bfloat16
f32 = jnp.float32


def dot_nn(a, b):
    return lax.dot_general(a, b, (((1,), (0,)), ((), ())), preferred_element_type=f32)


def dot_nt(a, b):
    return lax.dot_general(a, b, (((1,), (1,)), ((), ())), preferred_element_type=f32)


def dot_tn(a, b):
    return lax.dot_general(a, b, (((0,), (0,)), ((), ())), preferred_element_type=f32)


def encoder_bucket(offset):
    distance = np.abs(offset)
    bucket = np.minimum(distance, 8)
    for boundary in enc_edges:
        bucket = bucket + (distance >= boundary)
    return bucket + 16 * (offset > 0)


def decoder_bucket(offset):
    distance = np.maximum(-offset, 0)
    bucket = np.minimum(distance, 16)
    for boundary in dec_edges:
        bucket = bucket + (distance >= boundary)
    return bucket


def enc_offsets():
    lane = np.arange(WIDE)
    shifted = np.where(lane < BIG, lane, lane - WIDE)
    return 128 * np.arange(3)[:, None] - shifted[None, :]


def diagonal_offsets(rows, width):
    return rows - 1 - np.arange(width)


def dec_offsets():
    return np.arange(TGT)[:, None] - np.arange(TGT)[None, :]


def one_hot(bucket):
    return (bucket[..., None] == np.arange(NB)).astype(np.float32)


def spread_table(table, bucket):
    hot = jnp.asarray(one_hot(bucket))
    return jnp.sum(hot[None] * jnp.transpose(table).reshape((HEADS,) + (1,) * bucket.ndim + (NB,)), axis=-1)


def norm_scale(rows):
    return lax.rsqrt(jnp.mean(rows * rows, axis=-1, keepdims=True) + epsilon)


def norm_rows(rows, gain):
    return (rows * norm_scale(rows) * gain).astype(bf16)


def norm_back(rows, gain, grad):
    scale = norm_scale(rows)
    unit = rows * scale
    weighted = grad * gain
    grad_rows = scale * (weighted - unit * jnp.mean(weighted * unit, axis=-1, keepdims=True))
    return grad_rows, jnp.sum(grad * unit, axis=0, keepdims=True)


def gelu_both(u):
    root = np.float32(np.sqrt(2.0 / np.pi))
    cubic = np.float32(0.044715)
    square = u * u
    bend = jnp.tanh(u * (root + root * cubic * square))
    half = 0.5 * (1.0 + bend)
    slope = half + 0.5 * u * (1.0 - bend * bend) * (root + 3.0 * root * cubic * square)
    return (u * half).astype(bf16), slope.astype(bf16)


CORE, ACROSS, START, OWNER, BASE, PIECE = 0, 1, 2, 3, 6, 10


def shape(dims, dtype=bf16):
    return jax.ShapeDtypeStruct(dims, dtype)


def whole(*dims):
    return pl.BlockSpec(dims, lambda *_: (0,) * len(dims))


def call(kernel, grid, scalars, ins, outs, scratch=(), flops=10**10, aliases=None):
    return pl.pallas_call(
        kernel,
        grid_spec=pltpu.PrefetchScalarGridSpec(
            num_scalar_prefetch=1,
            grid=grid,
            in_specs=[spec for _, spec in ins],
            out_specs=tuple(spec for _, spec in outs),
            scratch_shapes=scratch,
        ),
        out_shape=tuple(kind for kind, _ in outs),
        input_output_aliases=aliases or {},
        compiler_params=pltpu.CompilerParams(vmem_limit_bytes=25 << 20),
        cost_estimate=pl.CostEstimate(flops=flops, bytes_accessed=1 << 20, transcendentals=0),
    )(scalars, *[array for array, _ in ins])


def lane_half(value, which):
    lane = lax.broadcasted_iota(jnp.int32, value.shape, 1)
    keep = (lane < HD) if which == 0 else (lane >= HD)
    return jnp.where(keep, value, jnp.zeros_like(value))


def softmax_t(scores):
    peak = jnp.max(scores, axis=0, keepdims=True)
    raised = jnp.exp(scores - peak)
    total = jnp.sum(raised, axis=0, keepdims=True)
    return (raised * (1.0 / total)).astype(bf16)


def toeplitz(row, rows):
    spread = jnp.broadcast_to(row, (rows, row.shape[-1]))
    return pltpu.roll(spread, 0, 1, stride=1, stride_axis=0)


def diagonals(value, width):
    rows = value.shape[0]
    row = lax.broadcasted_iota(jnp.int32, (rows, rows), 0)
    col = lax.broadcasted_iota(jnp.int32, (rows, rows), 1)
    flipped = dot_nn((row + col == rows - 1).astype(bf16), value)
    padded = jnp.concatenate([flipped, jnp.zeros((rows, width - value.shape[1]), f32)], axis=1)
    return jnp.sum(pltpu.roll(padded, 0, 1, stride=1, stride_axis=0), axis=0, keepdims=True)


def rest_mask():
    row = lax.broadcasted_iota(jnp.int32, (REST, REST), 0) // SMALL
    col = lax.broadcasted_iota(jnp.int32, (REST, REST), 1) // SMALL
    return row == col


def score_grad(weights, grad_weights, row_sum):
    return (weights.astype(f32) * (grad_weights - row_sum)).astype(bf16)


def transposed(value):
    return value.astype(f32).T.astype(bf16) if value.dtype == bf16 and value.shape[0] % 128 else value.T


def take_near(at, own, near, which):
    return jnp.where(which, own[0], near[0])


def attend_pair(q, k, v, bias_ref, big_ref, rest_ref):
    values_t = v.T
    allowed = rest_mask()
    heads = []
    for hh in range(2):
        queries = lane_half(q, hh)
        bias = [toeplitz(bias_ref[hh, b : b + 1, :], 128)[:, :BIG] for b in range(3)]
        scores = dot_nt(k[:BIG], queries[:BIG]) + jnp.concatenate(bias, axis=0)
        weights = softmax_t(scores)
        big_ref[hh] = weights
        head_v = values_t[hh * HD : (hh + 1) * HD]
        context = dot_nn(head_v[:, :BIG], weights)
        rest = dot_nt(k[BIG:], queries[BIG:]) + bias[0][:, :REST]
        rest = softmax_t(jnp.where(allowed, rest, masked_score))
        rest_ref[hh] = rest
        heads.append(jnp.concatenate([context, dot_nn(head_v[:, BIG:], rest)], axis=1))
    return jnp.concatenate(heads, axis=0).T.astype(bf16)


def enc_attention(scalars, rows, gains, bias, own, near, got, got_near, chunk):
    opening = chunk == 0
    quarter = got.shape[1]

    def kernel(at, rows_ref, gain_ref, bias_ref, oq, okv, nq, nkv, gw, gnw, *refs):
        if opening:
            qkv_ref, c_ref, big_ref, rest_ref, w_ref, n1_ref, xr_ref, twice = refs
            @pl.when(pl.program_id(0) == 0)
            def _():
                twice[:BUF] = rows_ref[0]
                twice[BUF:] = rows_ref[0, :REST]
                rolled = twice[pl.ds(pl.multiple_of(at[START], SMALL), BUF)]
                xr_ref[...] = rolled
                n1_ref[...] = norm_rows(rolled.astype(f32), gain_ref[0:1])
        else:
            qkv_ref, c_ref, big_ref, rest_ref, w_ref = refs
            n1_ref = rows_ref
        parts = ((oq[0], okv[0], okv[1]), (nq[0], nkv[0], nkv[1]), (gw[0], gw[1], gw[2]), (gnw[0], gnw[1], gnw[2]))
        for k, mats in enumerate(parts):
            place = pl.ds(pl.multiple_of(at[BASE + k], quarter), quarter)
            w_ref[0, place] = jnp.concatenate(mats, axis=1)
        qkv = dot_nn(n1_ref[...], w_ref[0]).astype(bf16)
        qkv_ref[0] = qkv
        c_ref[...] = attend_pair(qkv[:, :128], qkv[:, 128:256], qkv[:, 256:], bias_ref, big_ref, rest_ref)

    first = 3 * chunk
    one = pl.BlockSpec((1, quarter, 128), lambda p, at: (0, 0, first + p))
    two = pl.BlockSpec((2, quarter, 128), lambda p, at: (0, 0, first + p))
    three = pl.BlockSpec((3, quarter, 128), lambda p, at: (0, 0, p))
    rows_spec = pl.BlockSpec((1, BUF, D), lambda p, at: (at[CORE], 0, 0)) if opening else whole(BUF, D)
    outs = [
        (shape((3, BUF, 384)), pl.BlockSpec((1, BUF, 384), lambda p, at: (p, 0, 0))),
        (shape((BUF, 384)), pl.BlockSpec((BUF, 128), lambda p, at: (0, p))),
        (shape((6, BIG, BIG)), pl.BlockSpec((2, BIG, BIG), lambda p, at: (p, 0, 0))),
        (shape((6, REST, REST)), pl.BlockSpec((2, REST, REST), lambda p, at: (p, 0, 0))),
        (shape((3, D, 384)), pl.BlockSpec((1, D, 384), lambda p, at: (p, 0, 0))),
    ]
    if opening:
        outs += [(shape((BUF, D)), whole(BUF, D))] * 2
    return call(
        kernel, (3,), scalars,
        [
            (rows, rows_spec), (gains, whole(5, D)),
            (bias, pl.BlockSpec((2, 3, WIDE), lambda p, at: (first + p, 0, 0))),
            (own[0], one), (own[1], two), (near[0], one), (near[1], two), (got, three), (got_near, three),
        ],
        outs, [pltpu.VMEM((BUF + REST, D), bf16)] if opening else (), 2 * 10**10,
    )


FTILE = 384


def feed_specs(index, count):
    own = pl.BlockSpec((1, FTILE, D), lambda i, at: (index, jnp.minimum(i, count - 1), 0))
    near = pl.BlockSpec((1, FTILE, D), lambda i, at: (index, jnp.maximum(i - count, 0), 0))
    return own, near


def enc_feed(scalars, xr, c_a, c_b, own_o, near_o, got, got_near, gains, feed_in, near_in, feed_out, near_out):
    quarter = got.shape[0]
    count = feed_in.shape[1] // FTILE

    def kernel(at, xr_ref, ca, cb, oo, no, go, gno, gain_ref, fi, ni, fo, nf, h1_ref, n2_ref, a_ref, s_ref, p_ref, wo_ref, total):
        step = pl.program_id(0)

        @pl.when(step == 0)
        def _():
            for k, piece in enumerate((oo[0], no[0], go[...], gno[...])):
                wo_ref[pl.ds(pl.multiple_of(at[BASE + k], quarter), quarter)] = piece
            context = jnp.concatenate([ca[...], cb[...]], axis=1)
            h1 = (xr_ref[...].astype(f32) + dot_nn(context, wo_ref[...])).astype(bf16)
            h1_ref[...] = h1
            n2_ref[...] = norm_rows(h1.astype(f32), gain_ref[1:2])
            total[...] = jnp.zeros_like(total)

        w_in = jnp.where(step < count, fi[0], ni[0])
        w_out = jnp.where(step < count, fo[0], nf[0])
        a, slope = gelu_both(dot_nt(n2_ref[...], w_in))
        a_ref[...] = a
        s_ref[...] = slope
        total[...] += dot_nn(a, w_out)

        @pl.when(step == 2 * count - 1)
        def _():
            p_ref[...] = total[...].astype(bf16)

    own, near = feed_specs(0, count)
    rows = whole(BUF, D)
    tile = pl.BlockSpec((BUF, FTILE), lambda i, at: (0, i))
    quarter_spec = pl.BlockSpec((1, quarter, D), lambda i, at: (0, 0, 0))
    return call(
        kernel, (2 * count,), scalars,
        [
            (xr, rows), (c_a, whole(BUF, 384)), (c_b, whole(BUF, 384)), (own_o, quarter_spec), (near_o, quarter_spec),
            (got, whole(quarter, D)), (got_near, whole(quarter, D)), (gains, whole(5, D)),
            (feed_in, own), (near_in, near), (feed_out, own), (near_out, near),
        ],
        [
            (shape((BUF, D)), rows), (shape((BUF, D)), rows), (shape((BUF, 2 * count * FTILE)), tile),
            (shape((BUF, 2 * count * FTILE)), tile), (shape((BUF, D)), rows), (shape((D, D)), whole(D, D)),
        ],
        [pltpu.VMEM((BUF, D), f32)], 2 * 10**10,
    )


GROUP = 4
GROUPS = HEADS // GROUP
CROSS_KEYS = ((0, BIG), (BIG, BIG + SMALL), (BIG + SMALL, BUF))
SELF_KEYS = tuple((i * TGT, (i + 1) * TGT) for i in range(QPB))


def own_head(value):
    row = lax.broadcasted_iota(jnp.int32, value.shape, 0) // TGT
    lane = lax.broadcasted_iota(jnp.int32, value.shape, 1) // HD
    return jnp.where(row == lane, value, jnp.zeros_like(value))


def spread_heads(rows):
    return own_head(jnp.concatenate([rows] * GROUP, axis=0))


def join_heads(value):
    value = own_head(value)
    return sum(value[h * TGT : (h + 1) * TGT] for h in range(GROUP))


def turned(value):
    return value.astype(f32).T.astype(bf16)


def small_attend(keys_of, q, k, v, p_ref, bias_ref=None):
    contexts = []
    for group in range(GROUPS):
        lanes = slice(GROUP * HD * group, GROUP * HD * (group + 1))
        rows = []
        for i, (first, last) in enumerate(keys_of):
            scores = dot_nt(k[first:last, lanes], spread_heads(q[i * TGT : (i + 1) * TGT, lanes]))
            if bias_ref is not None:
                scores = scores + bias_ref[group]
            weights = softmax_t(scores)
            p_ref[group, first:last] = weights
            rows.append(join_heads(dot_nn(turned(weights), v[first:last, lanes])))
        contexts.append(jnp.concatenate(rows, axis=0))
    return jnp.concatenate(contexts, axis=1).astype(bf16)


def small_attend_back(keys_of, q, k, v, grads, p_ref, bias_ref=None):
    dq, dk, dv = [], [], []
    for group in range(GROUPS):
        lanes = slice(GROUP * HD * group, GROUP * HD * (group + 1))
        dq_rows, dk_rows, dv_rows = [], [], []
        bias_grad = 0.0
        for i, (first, last) in enumerate(keys_of):
            own = slice(i * TGT, (i + 1) * TGT)
            queries, out_grads = spread_heads(q[own, lanes]), spread_heads(grads[own, lanes])
            weights = p_ref[group, first:last]
            grad_weights = dot_nt(v[first:last, lanes], out_grads)
            row_sum = jnp.sum(weights.astype(f32) * grad_weights, axis=0, keepdims=True)
            ds = score_grad(weights, grad_weights, row_sum)
            dv_rows.append(dot_nn(weights, out_grads))
            dk_rows.append(dot_nn(ds, queries))
            dq_rows.append(join_heads(dot_nn(turned(ds), k[first:last, lanes])))
            if bias_ref is not None:
                bias_grad = bias_grad + ds.astype(f32)
        if bias_ref is not None:
            bias_ref[group] = bias_grad
        for to, parts in ((dq, dq_rows), (dk, dk_rows), (dv, dv_rows)):
            to.append(jnp.concatenate(parts, axis=0).astype(bf16))
    return tuple(jnp.concatenate(parts, axis=1) for parts in (dq, dk, dv))


def by_owner(at, ref):
    return jnp.concatenate(
        [ref[0, pl.ds(pl.multiple_of(at[OWNER + i] * TGT, TGT), TGT)] for i in range(QPB)], axis=0
    )


def core_rows():
    return pl.BlockSpec((1, DEC, D), lambda i, at: (at[CORE], 0, 0))


ANYWHERE = pl.BlockSpec(memory_space=pl.ANY)


def weight_args(parts):
    return [(array, ANYWHERE) for array in parts]


def weight_copies(at, index, refs, w, sem):
    quarter = refs[0].shape[1]
    pieces, piece = refs[6].shape[0], refs[6].shape[2]
    copies = []

    def copy(source, target):
        copies.append(pltpu.make_async_copy(source, target, sem.at[len(copies)]))

    for k in range(2):
        place = pl.ds(pl.multiple_of(at[BASE + k], quarter), quarter)
        q, kv, o = refs[3 * k : 3 * k + 3]
        copy(q.at[index], w.at[0, place])
        copy(kv.at[pl.ds(2 * index, 2)], w.at[pl.ds(1, 2), place])
        copy(o.at[index], w.at[3, place])
    for k in range(2):
        for j in range(pieces):
            row = at[BASE + 2 + k] + at[PIECE + 4 * (index - 1) + j]
            copy(refs[6 + k].at[j], w.at[:, pl.ds(pl.multiple_of(row, piece), piece)])
    for one in copies:
        one.start()
    return copies


WEIGHT_SCRATCH = [pltpu.VMEM((4, D, D), bf16), pltpu.SemaphoreType.DMA((14,))]


def dec_self(scalars, decoder_in, gains, bias, self_w):
    def kernel(at, x_ref, gain_ref, bias_ref, *refs):
        xd_ref, n3_ref, q_ref, k_ref, v_ref, c_ref, p_ref, m_ref, n4_ref, w, sem = refs[8:]
        copies = weight_copies(at, 1, refs[:8], w, sem)
        xd = by_owner(at, x_ref)
        xd_ref[...] = xd
        n3 = norm_rows(xd.astype(f32), gain_ref[2:3])
        n3_ref[...] = n3
        for one in copies:
            one.wait()
        q, k, v = (dot_nn(n3, w[i]).astype(bf16) for i in range(3))
        q_ref[...], k_ref[...], v_ref[...] = q, k, v
        c = small_attend(SELF_KEYS, q, k, v, p_ref, bias_ref)
        c_ref[...] = c
        m = xd.astype(f32) + dot_nn(c, w[3])
        m_ref[...] = m
        n4_ref[...] = norm_rows(m, gain_ref[3:4])

    rows = whole(DEC, D)
    low = (shape((DEC, D)), rows)
    return call(
        kernel, (1,), scalars,
        [(decoder_in, core_rows()), (gains, whole(5, D)), (bias, whole(GROUPS, TGT, GROUP * TGT))] + weight_args(self_w),
        [low] * 6 + [(shape((GROUPS, DEC, 128)), whole(GROUPS, DEC, 128)), (shape((DEC, D), f32), rows), low],
        WEIGHT_SCRATCH, 10**8,
    )


def dec_cross(scalars, h1, part, other, m, n4, cross_w, gains, cotangent, feed_in, near_in, feed_out, near_out):
    hidden = feed_in.shape[1]

    def kernel(
        at, h1_ref, p0, p1, m_ref, n4_ref, gain_ref, cot_ref, fi, ni, fo, nf, *refs
    ):
        e_ref, q_ref, k_ref, v_ref, c_ref, p_ref, g_ref, n5_ref, cot_out, a_ref, du_ref, dn_ref, o_ref = refs[8:21]
        w, w_sem, w_in, w_out, sem = refs[21:]
        first = weight_copies(at, 2, refs[:8], w, w_sem)
        copies = []
        for k, (own, near, to) in enumerate(((fi, ni, w_in), (fo, nf, w_out))):
            copies.append(pltpu.make_async_copy(own.at[1], to.at[pl.ds(0, hidden)], sem.at[2 * k]))
            copies.append(pltpu.make_async_copy(near.at[1], to.at[pl.ds(hidden, hidden)], sem.at[1 + 2 * k]))
        for copy in copies:
            copy.start()
        cot = by_owner(at, cot_ref)
        cot_out[...] = cot
        e = (h1_ref[...].astype(f32) + (p0[...].astype(f32) + p1[...].astype(f32))).astype(bf16)
        e_ref[...] = e
        for one in first:
            one.wait()
        k = dot_nn(e, w[1]).astype(bf16)
        v = dot_nn(e, w[2]).astype(bf16)
        q = dot_nn(n4_ref[...], w[0]).astype(bf16)
        q_ref[...], k_ref[...], v_ref[...] = q, k, v
        c = small_attend(CROSS_KEYS, q, k, v, p_ref)
        c_ref[...] = c
        g = (m_ref[...] + dot_nn(c, w[3])).astype(bf16)
        g_ref[...] = g
        n5 = norm_rows(g.astype(f32), gain_ref[4:5])
        n5_ref[...] = n5
        copies[0].wait()
        copies[1].wait()
        a, slope = gelu_both(dot_nt(n5, w_in[...]))
        a_ref[...] = a
        copies[2].wait()
        copies[3].wait()
        du = (slope.astype(f32) * dot_nt(cot, w_out[...])).astype(bf16)
        du_ref[...] = du
        dn_ref[...] = dot_nn(du, w_in[...]).astype(bf16)
        o_ref[...] = dot_nn(a, w_out[...]).astype(bf16)

    rows, small = whole(BUF, D), whole(DEC, D)
    big_low, low = (shape((BUF, D)), rows), (shape((DEC, D)), small)
    wide = (shape((DEC, 2 * hidden)), whole(DEC, 2 * hidden))
    return call(
        kernel, (1,), scalars,
        [
            (h1, rows), (part, rows), (other, rows), (m, small), (n4, small),
            (gains, whole(5, D)), (cotangent, core_rows()),
            (feed_in, ANYWHERE), (near_in, ANYWHERE), (feed_out, ANYWHERE), (near_out, ANYWHERE),
        ]
        + weight_args(cross_w),
        [
            big_low, low, big_low, big_low, low, (shape((GROUPS, BUF, 128)), whole(GROUPS, BUF, 128)),
            low, low, low, wide, wide, low, low,
        ],
        WEIGHT_SCRATCH
        + [
            pltpu.VMEM((2 * hidden, D), bf16), pltpu.VMEM((2 * hidden, D), bf16), pltpu.SemaphoreType.DMA((4,)),
        ],
        2 * 10**10,
    )


def feed_weights(scalars, lefts, right_rows, hidden):
    count = hidden // FTILE
    pairs = len(lefts)
    rows = lefts[0].shape[0]

    def kernel(at, *refs):
        step = pl.program_id(0)
        ins, outs = refs[: 2 * pairs], refs[2 * pairs :]
        for keep, to in ((step < count, outs[:pairs]), (step >= count, outs[pairs:])):

            @pl.when(keep)
            def _(to=to):
                for k in range(pairs):
                    to[k][...] = dot_nn(transposed(ins[2 * k][...]), ins[2 * k + 1][...]).astype(bf16)

    tile = pl.BlockSpec((rows, FTILE), lambda i, at: (0, i))
    ins = []
    for left, right in zip(lefts, right_rows):
        ins += [(left, tile), (right, whole(rows, D))]
    kind = shape((hidden, D))
    own = (kind, pl.BlockSpec((FTILE, D), lambda i, at: (jnp.minimum(i, count - 1), 0)))
    other = (kind, pl.BlockSpec((FTILE, D), lambda i, at: (jnp.maximum(i - count, 0), 0)))
    return call(
        kernel, (2 * count,), scalars, ins, [own] * pairs + [other] * pairs,
        flops=10**10,
    )


def cross_back(scalars, g, gains, p0, p1, cot, cross_w, q, k, v, weights, m):
    def kernel(
        at, g_ref, gain_ref, p0_ref, p1_ref, cot_ref, q_ref, k_ref, v_ref, p_ref, m_ref, *refs
    ):
        dg_ref, dq_ref, dk_ref, dv_ref, de_ref, gain_out, dm_ref, w, sem = refs[8:]
        copies = weight_copies(at, 2, refs[:8], w, sem)
        dn5 = p0_ref[...].astype(f32) + p1_ref[...].astype(f32)
        dg_rows, gain4 = norm_back(g_ref[...].astype(f32), gain_ref[4:5], dn5)
        dg = (dg_rows + cot_ref[...].astype(f32)).astype(bf16)
        dg_ref[...] = dg
        for one in copies:
            one.wait()
        dc = dot_nt(dg, w[3]).astype(bf16)
        dq, dk, dv = small_attend_back(CROSS_KEYS, q_ref[...], k_ref[...], v_ref[...], dc, p_ref)
        dq_ref[...], dk_ref[...], dv_ref[...] = dq, dk, dv
        de_ref[...] = (dot_nt(dk, w[1]) + dot_nt(dv, w[2])).astype(bf16)
        dm_rows, gain3 = norm_back(m_ref[...], gain_ref[3:4], dot_nt(dq, w[0]))
        dm_ref[...] = dm_rows + dg.astype(f32)
        gain_out[...] = jnp.concatenate([gain3, gain4], axis=0)

    rows, small = whole(BUF, D), whole(DEC, D)
    big_low, low = (shape((BUF, D)), rows), (shape((DEC, D)), small)
    return call(
        kernel, (1,), scalars,
        [
            (g, small), (gains, whole(5, D)), (p0, small), (p1, small), (cot, small),
            (q, small), (k, rows), (v, rows), (weights, whole(GROUPS, BUF, 128)), (m, small),
        ]
        + weight_args(cross_w),
        [low, low, big_low, big_low, big_low, (shape((2, D), f32), whole(2, D)), (shape((DEC, D), f32), small)],
        WEIGHT_SCRATCH,
        2 * 10**10,
    )


def enc_feed_back(scalars, de, slope, feed_in, near_in, feed_out, near_out):
    count = feed_in.shape[1] // FTILE

    def kernel(at, de_ref, s_ref, fi, ni, fo, nf, du_ref, p_ref, total):
        step = pl.program_id(0)
        w_in = jnp.where(step < count, fi[0], ni[0])
        w_out = jnp.where(step < count, fo[0], nf[0])
        du = (s_ref[...].astype(f32) * dot_nt(de_ref[...], w_out)).astype(bf16)
        du_ref[...] = du
        grad = dot_nn(du, w_in)

        @pl.when(step == 0)
        def _():
            total[...] = grad

        @pl.when(step > 0)
        def _():
            total[...] += grad

        @pl.when(step == 2 * count - 1)
        def _():
            p_ref[...] = total[...].astype(bf16)

    own, near = feed_specs(0, count)
    tile = pl.BlockSpec((BUF, FTILE), lambda i, at: (0, i))
    return call(
        kernel, (2 * count,), scalars,
        [(de, whole(BUF, D)), (slope, tile), (feed_in, own), (near_in, near), (feed_out, own), (near_out, near)],
        [(shape(slope.shape), tile), (shape((BUF, D)), whole(BUF, D))],
        [pltpu.VMEM((BUF, D), f32)], 2 * 10**10,
    )


def chip_cols(at, ref):
    return ref[:, pl.ds(pl.multiple_of(at[ACROSS] * BIG, 128), BIG)]


def store_rows(at, grads, own_ref, other_ref):
    first = at[CORE] == 0
    for i, grad in enumerate(grads):
        low = grad.astype(bf16)
        half = low.shape[0] // 2
        own_ref[i] = jnp.where(first, low[:half], low[half:])
        other_ref[i] = jnp.where(first, low[half:], low[:half])


def quarter_outs(mats):
    kind = (shape((mats, BIG // 2, D)), whole(mats, BIG // 2, D))
    return [kind, kind]


def cross_weights(scalars, n4, dq, e, dk, dv, c, dg):
    def kernel(at, n4_ref, dq_ref, e_ref, dk_ref, dv_ref, c_ref, dg_ref, own_ref, other_ref):
        n4_t, e_t, c_t = (transposed(chip_cols(at, ref)) for ref in (n4_ref, e_ref, c_ref))
        pairs = ((n4_t, dq_ref), (e_t, dk_ref), (e_t, dv_ref), (c_t, dg_ref))
        store_rows(at, [dot_nn(left, right[...]) for left, right in pairs], own_ref, other_ref)

    rows, small = whole(BUF, D), whole(DEC, D)
    return call(
        kernel, (1,), scalars,
        [(n4, small), (dq, small), (e, rows), (dk, rows), (dv, rows), (c, small), (dg, small)],
        quarter_outs(4),
    )


def self_back(scalars, dm, gains, self_w, q, k, v, c, weights, xd, n3):
    def kernel(at, dm_ref, gain_ref, q_ref, k_ref, v_ref, c_ref, p_ref, xd_ref, n3_ref, *refs):
        own_ref, other_ref, grad_ref, gain_out, diag_ref, w, sem = refs[8:]
        copies = weight_copies(at, 1, refs[:8], w, sem)
        dm = dm_ref[...]
        low = dm.astype(bf16)
        for one in copies:
            one.wait()
        dc = dot_nt(low, w[3]).astype(bf16)
        dq, dk, dv = small_attend_back(SELF_KEYS, q_ref[...], k_ref[...], v_ref[...], dc, p_ref, diag_ref)
        dn3 = dot_nt(dq, w[0]) + dot_nt(dk, w[1]) + dot_nt(dv, w[2])
        dd, gain2 = norm_back(xd_ref[...].astype(f32), gain_ref[2:3], dn3)
        gain_out[...] = gain2
        grad = (dd + dm).astype(bf16)
        for i in range(QPB):
            grad_ref[pl.ds(pl.multiple_of(at[OWNER + i] * TGT, TGT), TGT)] = grad[i * TGT : (i + 1) * TGT]
        n3_t, c_t = transposed(chip_cols(at, n3_ref)), transposed(chip_cols(at, c_ref))
        store_rows(at, [dot_nn(n3_t, dq), dot_nn(n3_t, dk), dot_nn(n3_t, dv), dot_nn(c_t, low)], own_ref, other_ref)

    small = whole(DEC, D)
    return call(
        kernel, (1,), scalars,
        [
            (dm, small), (gains, whole(5, D)),
            (q, small), (k, small), (v, small), (c, small), (weights, whole(GROUPS, DEC, 128)), (xd, small), (n3, small),
        ]
        + weight_args(self_w),
        quarter_outs(4)
        + [
            (shape((DEC, D)), small), (shape((1, D), f32), whole(1, D)),
            (shape((GROUPS, TGT, 128), f32), whole(GROUPS, TGT, 128)),
        ],
        WEIGHT_SCRATCH, 10**9,
    )


def enc_back(scalars, opening, gains, xr, chunk, chunk_c, n1=None, start=None, carried=None):
    half = BIG // 2
    first = 0 if opening else 3

    def kernel(at, gain_ref, xr_ref, wo_ref, ca_ref, cb_ref, qkv_ref, c_ref, big_ref, rest_ref, w_ref, *refs):
        if opening:
            h1_ref, p0_ref, p1_ref, de_ref, n1_ref = refs[:5]
            own_ref, other_ref, diag_ref, rdiag_ref, dh1_ref, dn1_ref, n1_t, c_t, gain_out = refs[5:]
        else:
            dh1_ref, dn1_in, n1_t, c_t = refs[:4]
            own_ref, other_ref, diag_ref, rdiag_ref, grad_ref, gain_out, dn1_ref, twice = refs[6:]
        p = pl.program_id(0)

        @pl.when(p == 0)
        def _():
            if opening:
                dn2 = p0_ref[...].astype(f32) + p1_ref[...].astype(f32)
                dh1_rows, gain1 = norm_back(h1_ref[...].astype(f32), gain_ref[1:2], dn2)
                dh1_ref[...] = (dh1_rows + de_ref[...].astype(f32)).astype(bf16)
                gain_out[...] = gain1
                n1_t[...] = chip_cols(at, n1_ref).T
                c_t[...] = jnp.where(at[ACROSS] == 0, ca_ref[...], cb_ref[...]).T
                dn1_ref[...] = jnp.zeros_like(dn1_ref)
            else:
                dn1_ref[...] = dn1_in[...]

        qkv, c, w = qkv_ref[0], c_ref[...], w_ref[0]
        q, k, v = qkv[:, :128], qkv[:, 128:256], qkv[:, 256:]
        dh1 = dh1_ref[...]
        grads = dot_nt(dh1, wo_ref[...]).astype(bf16)
        keys_t = k.T
        product_t = (grads.astype(f32) * c.astype(f32)).T
        dq_t = []
        dk_big = dv_big = dk_rest = dv_rest = 0.0
        for hh in range(2):
            row_sum = jnp.sum(product_t[hh * HD : (hh + 1) * HD], axis=0, keepdims=True)
            queries, values, grads_h = lane_half(q, hh), lane_half(v, hh), lane_half(grads, hh)
            head_k = keys_t[hh * HD : (hh + 1) * HD]
            weights = big_ref[hh]
            ds = score_grad(weights, dot_nt(values[:BIG], grads[:BIG]), row_sum[:, :BIG])
            dv_big = dv_big + dot_nn(weights, grads_h[:BIG])
            dk_big = dk_big + dot_nn(ds, queries[:BIG])
            diag_ref[hh] = jnp.concatenate(
                [diagonals(ds[128 * b : 128 * (b + 1)], WIDE) for b in range(3)], axis=0
            )
            dq_head = dot_nn(head_k[:, :BIG], ds)
            weights = rest_ref[hh]
            ds = score_grad(weights, dot_nt(values[BIG:], grads[BIG:]), row_sum[:, BIG:])
            dv_rest = dv_rest + dot_nn(weights, grads_h[BIG:])
            dk_rest = dk_rest + dot_nn(ds, queries[BIG:])
            rdiag_ref[hh] = diagonals(ds, 2 * REST)
            dq_t.append(jnp.concatenate([dq_head, dot_nn(head_k[:, BIG:], ds)], axis=1))
        dq = jnp.concatenate(dq_t, axis=0).T.astype(bf16)
        dk = jnp.concatenate([dk_big, dk_rest], axis=0).astype(bf16)
        dv = jnp.concatenate([dv_big, dv_rest], axis=0).astype(bf16)
        dqkv = jnp.concatenate([dq, dk, dv], axis=1)
        dn1_ref[...] += dot_nt(dqkv, w)
        grad = dot_nn(n1_t[...], dqkv)
        columns = pl.ds(pl.multiple_of(128 * (first + p), 128), 128)
        out_grad = dot_nn(c_t[...], dh1_ref[:, columns])
        store_rows(at, [grad[:, 128 * i : 128 * i + 128] for i in range(3)] + [out_grad], own_ref, other_ref)

        if not opening:

            @pl.when(p == 2)
            def _():
                rows, gain0 = norm_back(xr_ref[...].astype(f32), gain_ref[0:1], dn1_ref[...])
                gain_out[...] = gain0
                low = (rows + dh1.astype(f32)).astype(bf16)
                twice[:BUF] = low
                twice[BUF:] = low
                grad_ref[...] = twice[pl.ds(pl.multiple_of(BUF - at[START], SMALL), BUF)]

    rows = whole(BUF, D)
    wo = start[4] if opening else carried[-1]
    qkv, c, big, rest, w = chunk
    ins = [
        (gains, whole(5, D)), (xr, rows), (wo, pl.BlockSpec((128, D), lambda p, at: (first + p, 0))),
        (chunk_c[0], whole(BUF, BIG)), (chunk_c[1], whole(BUF, BIG)),
        (qkv, pl.BlockSpec((1, BUF, BIG), lambda p, at: (p, 0, 0))),
        (c, pl.BlockSpec((BUF, 128), lambda p, at: (0, p))),
        (big, pl.BlockSpec((2, BIG, BIG), lambda p, at: (p, 0, 0))),
        (rest, pl.BlockSpec((2, REST, REST), lambda p, at: (p, 0, 0))),
        (w, pl.BlockSpec((1, D, BIG), lambda p, at: (p, 0, 0))),
    ]
    columns = (shape((4, half, D)), pl.BlockSpec((4, half, 128), lambda p, at: (0, 0, first + p)))
    outs = [
        columns, columns,
        (shape((6, 3, WIDE), f32), pl.BlockSpec((2, 3, WIDE), lambda p, at: (p, 0, 0))),
        (shape((6, 1, 2 * REST), f32), pl.BlockSpec((2, 1, 2 * REST), lambda p, at: (p, 0, 0))),
    ]
    low, turned = (shape((BUF, D)), rows), (shape((BIG, BUF)), whole(BIG, BUF))
    one = (shape((1, D), f32), whole(1, D))
    scratch, aliases = (), {}
    if opening:
        ins += [(value, rows) for value in start[:4]] + [(n1, rows)]
        outs += [low, (shape((BUF, D), f32), rows), turned, turned, one]
    else:
        own, other, dh1, dn1, n1_t, c_t, _ = carried
        ins += [(dh1, rows), (dn1, rows), (n1_t, whole(BIG, BUF)), (c_t, whole(BIG, BUF)), (own, ANYWHERE), (other, ANYWHERE)]
        aliases = {len(ins) - 1: 0, len(ins): 1}
        outs += [low, one]
        scratch = [pltpu.VMEM((BUF, D), f32), pltpu.VMEM((2 * BUF, D), bf16)]
    return call(kernel, (3,), scalars, ins, outs, scratch, 2 * 10**10, aliases)


def swap_section(value, bit):
    count = lax.axis_size("section")
    return lax.ppermute(value, "section", [(i, i ^ bit) for i in range(count)])


def swap_dp(value, bit):
    count = lax.axis_size("dp")
    return lax.ppermute(value, "dp", [(i, i ^ bit) for i in range(count)])


def add_low(a, b):
    return (a.astype(f32) + b.astype(f32)).astype(bf16)


def tie(value, *deps):
    return lax.optimization_barrier((value,) + deps)[0] if deps else value


def halves(own, got, extra=None):
    half = own.shape[0] // 2
    mine = lax.axis_index("dp") % 2

    def part(which):
        rows = [lax.dynamic_slice_in_dim(value, which * half, half, 0) for value in (own, got)]
        total = add_low(*rows)
        return total if extra is None else jnp.concatenate([total, extra])

    return part(mine), part(1 - mine)


def rejoin(keep, other):
    mine = lax.axis_index("dp") % 2
    keep = keep[: other.shape[0]]
    return jnp.where(mine == 0, jnp.concatenate([keep, other]), jnp.concatenate([other, keep]))


Y_TIME, TREE_TIME, STEP = 12.7, 12.7, 3.0
STAGES = (("y", Y_TIME), ("in", TREE_TIME), ("mid", TREE_TIME), ("out", TREE_TIME), ("y", Y_TIME))
ROUTES = {
    "y": tuple((i, i ^ 1) for i in range(8)),
    "in": ((0, 2), (1, 3), (6, 4), (7, 5)),
    "mid": ((2, 4), (3, 5), (4, 2), (5, 3)),
    "out": ((2, 0), (3, 1), (4, 6), (5, 7)),
}


class GradSum:
    def __init__(self, pieces):
        self.count = lax.axis_size("dp")
        self.value = {}
        self.extra = None
        self.stage = {i: 0 for i in pieces}
        self.links = {name: [] for name in ROUTES}
        self.sent, self.got = {}, {}

    def enter(self, i, own, got, extra=None):
        own, got = own.reshape(-1, D), got.reshape(-1, D)
        if self.count != 8:
            self.value[i] = lax.psum(add_low(own, got), "dp")
            self.extra = None if extra is None else lax.psum(extra, "dp")
        else:
            self.value[i] = (own, got, extra)

    def step(self, i, *after):
        now = self.stage[i]
        self.stage[i] = now + 1
        if self.count != 8:
            return
        link = STAGES[now][0]
        value = self.value[i]
        if now > 0:
            value = tie(value, *after)
        if now == 0:
            value, sent = halves(*(tie(value[0], *after), tie(value[1], *after), value[2]))
        elif now == 4:
            sent = value[: value.shape[0] // 128 * 128]
            if sent.shape != value.shape:
                self.extra = value[sent.shape[0] :]
        else:
            sent = value
        before = self.links[link]
        sent = tie(sent, *before[-2:-1])
        got = lax.ppermute(sent, "dp", ROUTES[link])
        before.append(got)
        z = lax.axis_index("dp") // 2
        if now < 3:
            value = add_low(value, got)
        elif now == 3:
            value = jnp.where((z == 0) | (z == 3), got, value)
        else:
            value = rejoin(value, got)
        self.value[i], self.sent[i, now], self.got[i, now] = value, sent, got

    def between(self, after, ended, begun):
        for i in begun:
            self.step(i, after)
        if self.count != 8:
            return []
        return [self.got[key] for key in ended] + [self.sent[i, self.stage[i] - 1] for i in begun]

    def finish(self, late):
        free = {name: 0.0 for name in ROUTES}
        at = {i: late.get(i, 0.0) for i in self.stage}
        while min(self.stage.values()) < len(STAGES):
            best = None
            for i, now in self.stage.items():
                if now < len(STAGES):
                    key = (max(at[i], free[STAGES[now][0]]), now - len(STAGES), i)
                    best = key if best is None else min(best, key)
            begin, _, i = best
            link, length = STAGES[self.stage[i]]
            free[link], at[i] = begin + length + 0.5, begin + length + STEP
            self.step(i)
        return self.value


def shards(
    encoder_in, decoder_in, lengths, query_map, attn_query, attn_keyval, attn_output,
    feed_in, feed_out, norm_gains, position_bias, cotangent,
):
    section_id = lax.axis_index("section")
    across = section_id // 2
    core = section_id % 2
    quarter = attn_query.shape[1]
    half = 2 * quarter

    dp_id = lax.axis_index("dp")
    own = (attn_query, attn_keyval, attn_output)
    near = tuple(swap_section(a, 1) for a in own)
    hidden = feed_in.shape[1]

    def packed(index, mats, first, last, *after):
        parts = [tie(attn_query[index : index + 1], *after), attn_keyval[2 * index : 2 * index + 2], attn_output[index : index + 1]]
        return jnp.concatenate(parts[: mats - 1], axis=0)[:, :, first:last]

    bases = [(section_id ^ k) * quarter for k in range(4)]
    def piece_of(index, count, *after):
        size = quarter // count
        piece = lax.dynamic_slice_in_dim(packed(index, 4, 0, D), (dp_id % count) * size, size, 1)
        return swap_section(tie(piece, *after), 2)

    def places(count):
        at = dp_id % count
        return [(at ^ k) * (quarter // count) if k < count else 0 for k in range(4)]

    pack_a = packed(0, 3, 0, D // 2)
    got_a = swap_section(pack_a, 2)

    big = jnp.argmax(lengths[core]).astype(jnp.int32)
    owners = lax.dynamic_slice_in_dim(jnp.concatenate([query_map[core]] * 2), big, QPB, 0)
    scalars = jnp.concatenate(
        [jnp.stack([core, across, big * SMALL]), owners, jnp.stack(bases + places(4) + places(2))]
    ).astype(jnp.int32)

    enc_table = spread_table(position_bias[0], encoder_bucket(enc_offsets()))
    causal = jnp.asarray(dec_offsets() <= 0)
    dec_table = jnp.where(causal, spread_table(position_bias[1], decoder_bucket(dec_offsets())), masked_score)
    dec_table = jnp.transpose(dec_table.reshape(GROUPS, GROUP, TGT, TGT), (0, 2, 1, 3)).reshape(GROUPS, TGT, GROUP * TGT)
    sums = GradSum(range(7))

    near_a = swap_section(tie(got_a, scalars, enc_table, dec_table), 1)
    got_b = swap_section(packed(0, 3, D // 2, D, pack_a), 2)
    got_self = piece_of(1, 4, near_a)
    first = enc_attention(scalars, encoder_in, norm_gains, enc_table, own, near, got_a, near_a, 0)
    n1, xr = first[5:]
    got_o = swap_section(tie(attn_output[0], near_a), 2)
    near_b = swap_section(tie(got_b, n1), 1)
    got_cross = piece_of(2, 2, n1)
    piece = tie(got_self, n1)
    second_piece, third_piece = swap_dp(piece, 1), swap_dp(piece, 2)
    near_in = swap_section(tie(feed_in, near_a), 1)
    near_out = swap_section(tie(feed_out, near_a), 1)
    second = enc_attention(scalars, n1, norm_gains, enc_table, own, near, got_b, near_b, 1)
    near_got_o = swap_section(tie(got_o, second[1]), 1)
    fourth_piece = swap_dp(tie(second_piece, second[1]), 2)
    quad = jnp.stack([piece, second_piece, third_piece, fourth_piece])
    h1, n2, a1, slope1, part, wo = enc_feed(
        scalars, xr, first[1], second[1], attn_output, near[2], got_o, near_got_o, norm_gains,
        feed_in, near_in, feed_out, near_out,
    )
    part_other = swap_section(part, 2)
    quad = tie(quad, part)
    self_w = own + near + (quad, swap_section(quad, 1))
    pair = tie(got_cross, second[1])
    pair = tie(jnp.stack([pair, swap_dp(pair, 1)]), part)
    cross_w = own + near + (pair, swap_section(pair, 1))
    xd, n3, q2, k2, v2, c2, p2, m, n4 = dec_self(scalars, decoder_in, norm_gains, dec_table, self_w)
    e, q3, k3, v3, c3, p3, g, n5, cot, a2, du2, dn5, out_part = dec_cross(
        scalars, h1, part, part_other, m, n4, cross_w, norm_gains, cotangent, feed_in, near_in, feed_out, near_out
    )

    dn5_other = swap_section(dn5, 2)
    own_out, own_in, other_out, other_in = feed_weights(scalars, (a2, du2), (cot, n5), hidden)
    sums.enter(0, own_out, swap_section(other_out, 1))
    sums.enter(1, own_in, swap_section(other_in, 1))

    dn5_other = tie(dn5_other, *sums.between(own_in, (), (0,)))
    dg, dq3, dk3, dv3, de, gains34, dm = cross_back(
        scalars, g, norm_gains, dn5, dn5_other, cot, cross_w, q3, k3, v3, p3, m
    )
    de = tie(de, *sums.between(dq3, (), (1,)))
    du1, dn2 = enc_feed_back(scalars, de, slope1, feed_in, near_in, feed_out, near_out)
    dn2_other = swap_section(dn2, 2)
    own_w, other_w = cross_weights(scalars, n4, dq3, e, dk3, dv3, c3, tie(dg, dn2))
    sums.enter(2, own_w, swap_section(other_w, 1))

    dm = tie(dm, own_w, *sums.between(own_w, (), (0,)))
    own_w, other_w, dec_grad, gain2, diag2 = self_back(scalars, dm, norm_gains, self_w, q2, k2, v2, c2, p2, xd, n3)
    sums.enter(5, own_w, swap_section(other_w, 1))

    n2_late = tie(n2, own_w, dn2_other, *sums.between(dec_grad, (), (1, 2)))
    own_out, own_in, other_out, other_in = feed_weights(scalars, (a1, du1), (de, n2_late), hidden)
    sums.enter(3, own_out, swap_section(other_out, 1))
    sums.enter(4, own_in, swap_section(other_in, 1))

    dn2_late = tie(dn2_other, own_in, *sums.between(own_in, (), (5, 0)))
    contexts = (first[1], second[1])
    own_w, other_w, diag_a, rdiag_a, dh1, dn1, n1_t, c_t, gain1 = enc_back(
        scalars, True, norm_gains, xr, first[:5], contexts, n1, (h1, dn2, dn2_late, de, wo)
    )
    dn1 = tie(dn1, *sums.between(dh1, (), (3, 1)))
    own_enc, other_w, diag_b, rdiag_b, enc_grad, gain0 = enc_back(
        scalars, False, norm_gains, xr, second[:5], contexts, carried=(own_w, other_w, dh1, dn1, n1_t, c_t, wo)
    )
    got_w = swap_section(other_w, 1)

    hot_enc = jnp.asarray(
        np.concatenate(
            [one_hot(encoder_bucket(128 * b + diagonal_offsets(128, WIDE))) for b in range(3)]
            + [one_hot(encoder_bucket(diagonal_offsets(REST, 2 * REST)))]
        )
    )
    hot_dec = jnp.asarray(one_hot(decoder_bucket(dec_offsets())))
    sums_enc = jnp.concatenate(
        [
            jnp.concatenate([d.reshape(HEADS // 2, -1), r.reshape(HEADS // 2, -1)], axis=1)
            for d, r in ((diag_a, rdiag_a), (diag_b, rdiag_b))
        ]
    )
    exact = lax.Precision.HIGHEST
    table_enc = jnp.einsum("mb,hm->bh", hot_enc, sums_enc, precision=exact)
    diag2 = diag2.reshape(GROUPS, TGT, GROUP, TGT)
    table_dec = jnp.einsum("kqb,gkhq->bgh", hot_dec, diag2, precision=exact).reshape(NB, HEADS)
    tables = jnp.stack([table_enc, table_dec]).reshape(-1, D)
    small = jnp.concatenate([gain0, gain1, gain2, gains34, tables, jnp.zeros((10, D), f32)])
    small = small + swap_section(small, 1)
    sums.enter(6, own_enc, got_w, small.astype(bf16))
    total = sums.finish({6: 6.0})
    unit_out2, unit_in2, unit_cross, unit_out1, unit_in1, unit_self, unit_enc = (total[i] for i in range(7))
    small = sums.extra.astype(f32)
    gains = small[:5]
    tables = small[5].reshape(2, NB, HEADS)

    def split_rows(rows, count):
        mine = lax.dynamic_slice_in_dim(rows, section_id * count, count, 0)
        theirs = swap_section(lax.dynamic_slice_in_dim(rows, (section_id ^ 1) * count, count, 0), 1)
        return jnp.where(core == 0, jnp.stack([mine, theirs]), jnp.stack([theirs, mine]))

    out_rows = (g.astype(f32) + (out_part.astype(f32) + swap_section(out_part, 2).astype(f32))).astype(bf16)
    restored = jnp.zeros((DEC, D), bf16)
    for i in range(QPB):
        restored = lax.dynamic_update_slice_in_dim(restored, out_rows[i * TGT : (i + 1) * TGT], owners[i] * TGT, 0)
    sections = lax.axis_size("section")
    decoder_out = split_rows(restored, DEC // sections)
    decoder_in_grad = split_rows(dec_grad, DEC // sections)
    encoder_in_grad = split_rows(enc_grad, BUF // sections)

    u_enc, u_self, u_cross = (
        u.reshape(4, quarter, D).astype(f32) for u in (unit_enc, unit_self, unit_cross)
    )
    query_grad = jnp.stack([u_enc[0], u_self[0], u_cross[0]])
    keyval_grad = jnp.concatenate([u_enc[1:3], u_self[1:3], u_cross[1:3]])
    output_grad = jnp.stack([u_enc[3], u_self[3], u_cross[3]])
    feed_in_grad = jnp.stack([unit_in1, unit_in2]).astype(f32)
    feed_out_grad = jnp.stack([unit_out1, unit_out2]).astype(f32)
    return (
        decoder_out, encoder_in_grad, decoder_in_grad, query_grad, keyval_grad, output_grad,
        feed_in_grad, feed_out_grad, gains, tables,
    )


def solution(mesh):
    rows = P("dp", None, None)
    mats = P(None, "section", None)
    outs = P("dp", "section", None)
    return jax.shard_map(
        shards,
        mesh=mesh,
        in_specs=(rows, rows, P("dp", None), P("dp", None), mats, mats, mats, mats, mats, P(), P(), rows),
        out_specs=(outs, outs, outs, mats, mats, mats, mats, mats, P(), P()),
        check_vma=False,
    )
```

profile of v0, /device:TPU:0, one launch (start us, length us, event | category | flops | bytes accessed | tf_op | source)
XLA Modules:
  0.0 400.0 jit_solution(12885122410675685824)
XLA Ops:
  26.1 8.7 %shard_map.240 = (bf16[3,512,384]{2,1,0:T(8,128)(2,1)S(1)}, bf16[512,384]{1,0:T(8,128)(2,1)S(1)}, bf16[6,384,384]{2,1,0:T(8,128)(2,1)S(1)}, bf16[6,128,128]{2,1,...) custom-call(s32[18]{0:T(128)S(1)} %concatenate.154.at, ...), custom_call_target="tpu_custom_call" | custom-call | flops 20000000000 | bytes 1048576 | tf_op jit(solution)/shard_map/pallas_call | solution.py:121
  46.4 4.8 %collective-permute-done.7.go = bf16[192,768]{1,0:T(8,128)(2,1)} collective-permute-done((bf16[192,768]{1,0:T(8,128)(2,1)}, bf16[192,768]{1,0:T(8,128)(2,1)}, u32[]{:S(2)}, u32[]{:S(2)}) %collective-permute-start.7) | collective-permute-done | bytes 294944 | tf_op jit(solution)/shard_map/ppermute | solution.py:781
  54.9 8.7 %shard_map.241 = (bf16[3,512,384]{2,1,0:T(8,128)(2,1)S(1)}, bf16[512,384]{1,0:T(8,128)(2,1)S(1)}, bf16[6,384,384]{2,1,0:T(8,128)(2,1)S(1)}, bf16[6,128,128]{2,1,0:T(8,128)(2,1)S(1)}, bf16[3,768,384]{2,1,0:T(8,128)(2,1)S(1)}) custom-call(s32[18]{0:T(128)S(1)} %concatenate.154.at, bf16[512,768]{1,0:T(8,128)(2,1)S(1)} %copy-done.115, f32[5,768]{1,0:T(8,128)S(1)} %copy-done.44, ...), custom_call_target="tpu_custom_call" | custom-call | flops 20000000000 | bytes 1048576 | tf_op jit(solution)/shard_map/pallas_call | solution.py:121
  68.7 6.0 %collective-permute-done.15 = bf16[4,48,768]{2,1,0:T(8,128)(2,1)S(1)} collective-permute-done((bf16[4,48,768]{2,1,0:T(8,128)(2,1)}, bf16[4,48,768]{2,1,0:T(8,128)(2,1)S(1)}, u32[]{:S(2)}, u32[]{:S(2)}) %collective-permute-start.15) | collective-permute-done | bytes 294944 | tf_op jit(solution)/shard_map/ppermute | solution.py:786
  78.0 9.3 %shard_map.242 = (bf16[512,768]{1,0:T(8,128)(2,1)S(1)}, bf16[512,768]{1,0:T(8,128)(2,1)S(1)}, bf16[512,1536]{1,0:T(8,128)(2,1)S(1)}, bf16[512,1536]{1,0:T(8,128)...) custom-call(s32[18]{0:T(128)S(1)} %concatenate.154.at, bf16[512,768]{1,0:T(8,128)(2,1)S(1)} %copy-done.112, ...), custom_call_target="tpu_custom_call" | custom-call | flops 20000000000 | bytes 1048576 | tf_op jit(solution)/shard_map/pallas_call | solution.py:121
  92.8 4.2 %shard_map.243 = (bf16[96,768]{1,0:T(8,128)(2,1)S(1)}, bf16[96,768]{1,0:T(8,128)(2,1)S(1)}, bf16[96,768]{1,0:T(8,128)(2,1)S(1)}, bf16[96,768]{1,0:T(8,128)(2,1)S...) custom-call(s32[18]{0:T(128)S(1)} %concatenate.154.at, ...), custom_call_target="tpu_custom_call" | custom-call | flops 100000000 | bytes 1048576 | tf_op jit(solution)/shard_map/pallas_call | solution.py:121
  101.0 10.2 %collective-permute-done.11.p1 = bf16[512,768]{1,0:T(8,128)(2,1)S(1)} collective-permute-done((bf16[512,768]{1,0:T(8,128)(2,1)S(1)}, bf16[512,768]{1,0:T(8,128)(2,1)S(1)}, u32[]{:S(2)}, u32[]{:S(2)}) %collective-permute-start.11) | collective-permute-done | bytes 786464 | tf_op jit(solution)/shard_map/ppermute | solution.py:781
  111.2 9.6 %shard_map.244 = (bf16[512,768]{1,0:T(8,128)(2,1)S(1)}, bf16[96,768]{1,0:T(8,128)(2,1)S(1)}, bf16[512,768]{1,0:T(8,128)(2,1)S(1)}, bf16[512,768]{1,0:T(8,128)(2,...) custom-call(s32[18]{0:T(128)S(1)} %concatenate.154.at, ...), custom_call_target="tpu_custom_call" | custom-call | flops 20000000000 | bytes 1048576 | tf_op jit(solution)/shard_map/pallas_call | solution.py:121
  120.9 3.7 shard_map.245
  147.8 6.8 %shard_map.246 = (bf16[96,768]{1,0:T(8,128)(2,1)S(1)}, bf16[96,768]{1,0:T(8,128)(2,1)S(1)}, bf16[512,768]{1,0:T(8,128)(2,1)S(1)}, bf16[512,768]{1,0:T(8,128)(2,1...) custom-call(s32[18]{0:T(128)S(1)} %concatenate.154.at, ...), custom_call_target="tpu_custom_call" | custom-call | flops 20000000000 | bytes 1048576 | tf_op jit(solution)/shard_map/pallas_call | solution.py:121
  157.2 6.3 %shard_map.247 = (bf16[512,1536]{1,0:T(8,128)(2,1)S(1)}, bf16[512,768]{1,0:T(8,128)(2,1)S(1)}) custom-call(s32[18]{0:T(128)S(1)} %concatenate.154.at, bf16[512,768]{1,0:T(8,128)(2,1)S(1)} %get-tuple-element.206.de_ref.refs_1_.refs_3_, bf16[512,1536]{1,0:T(8,128)(2,1)S(1)} %copy-done.98, bf16[2,768,768]{2,1,0:T(8,128)(2,1)S(1)} %copy-done.56, ...), custom_call_target="tpu_custom_call" | custom-call | flops 20000000000 | bytes 1048576 | tf_op jit(solution)/shard_map/pallas_call | solution.py:121
  171.2 3.8 add_convert_fusion.29
  175.0 3.2 collective-permute-start.30
  178.2 7.1 %shard_map.249 = (bf16[4,192,768]{2,1,0:T(8,128)(2,1)S(1)}, bf16[4,192,768]{2,1,0:T(8,128)(2,1)}, bf16[96,768]{1,0:T(8,128)(2,1)S(1)}, f32[1,768]{1,0:T(1,128)S(1)}, f32[3,32,128]{2,1,0:T(8,128)S(1)}) custom-call(s32[18]{0:T(128)S(1)} %concatenate.154.at, f32[96,768]{1,0:T(8,128)S(1)} %get-tuple-element.221.dm_ref, f32[5,768]{1,0:T(8,128)S(1)} %copy-done.46, ...), custom_call_target="tpu_custom_call" | custom-call | flops 1000000000 | bytes 1048576 | tf_op jit(solution)/shard_map/pallas_call | solution.py:121
  199.4 4.2 %shard_map.250 = (bf16[768,768]{1,0:T(8,128)(2,1)S(1)}, bf16[768,768]{1,0:T(8,128)(2,1)S(1)}, bf16[768,768]{1,0:T(8,128)(2,1)S(1)}, bf16[768,768]{1,0:T(8,128)(2,1)S(1)}) custom-call(s32[18]{0:T(128)S(1)} %concatenate.154.at, bf16[512,1536]{1,0:T(8,128)(2,1)S(1)} %copy-done.79, bf16[512,768]{1,0:T(8,128)(2,1)S(1)} %copy-done.85, ...), custom_call_target="tpu_custom_call" | custom-call | flops 10000000000 | bytes 1048576 | tf_op jit(solution)/shard_map/pallas_call | solution.py:121
  210.9 11.5 %shard_map.251 = (bf16[4,192,768]{2,1,0:T(8,128)(2,1)S(1)}, bf16[4,192,768]{2,1,0:T(8,128)(2,1)S(1)}, f32[6,3,512]{2,1,0:T(4,128)S(1)}, f32[6,1,256]{2,1,0:T(1,1...) custom-call(s32[18]{0:T(128)S(1)} %concatenate.154.at, ...), custom_call_target="tpu_custom_call" | custom-call | flops 20000000000 | bytes 1048576 | tf_op jit(solution)/shard_map/pallas_call | solution.py:121
  224.6 5.0 %collective-permute-start.43 = (bf16[384,768]{1,0:T(8,128)(2,1)}, bf16[384,768]{1,0:T(8,128)(2,1)}, u32[]{:S(2)}, u32[]{:S(2)}) collective-permute-start(bf16[384,768]{1,0:T(8,128)(2,1)} %add_convert_fusion.17), channel_id=1, source_target_pairs={{0,8},{4,12},{24,16},{28,20},{1,9},{5,13},{25,17},{29,21},{2,10},{... | collective-permute-start | bytes 1769480 | tf_op jit(solution)/shard_map/ppermute | solution.py:861
  233.9 9.7 %shard_map.252 = (bf16[4,192,768]{2,1,0:T(8,128)(2,1)S(1)}, bf16[4,192,768]{2,1,0:T(8,128)(2,1)S(1)}, f32[6,3,512]{2,1,0:T(4,128)S(1)}, f32[6,1,256]{2,1,0:T(1,1...) custom-call(s32[18]{0:T(128)S(1)} %concatenate.154.at, ...), custom_call_target="tpu_custom_call", output_to_operand_aliasing={{0}: (15, {}), {1}: (16, {})} | custom-call | flops 20000000000 | bytes 1048576 | tf_op jit(solution)/shard_map/pallas_call | solution.py:121
  261.7 7.6 %collective-permute-start.58 = (bf16[384,768]{1,0:T(8,128)(2,1)S(1)}, bf16[384,768]{1,0:T(8,128)(2,1)S(1)}, u32[]{:S(2)}, u32[]{:S(2)}) collective-permute-start(bf16[384,768]{1,0:T(8,128)(2,1)S(1)} %add_convert_fusion.8), channel_id=1, source_target_pairs={{0,8},{4,12},{24,16},{28,20},{1,9},{5,13},{25,17},{29,21},{2,10},{... | collective-permute-start | bytes 1769480 | tf_op jit(solution)/shard_map/ppermute | solution.py:861
  273.3 3.0 collective-permute-done.63
  276.3 4.1 %collective-permute-start.44 = (bf16[384,768]{1,0:T(8,128)(2,1)S(1)}, bf16[384,768]{1,0:T(8,128)(2,1)S(1)}, u32[]{:S(2)}, u32[]{:S(2)}) collective-permute-start(bf16[384,768]{1,0:T(8,128)(2,1)S(1)} %add_convert_fusion.19), channel_id=1, source_target_pairs={{0,8},{4,12},{24,16},{28,20},{1,9},{5,13},{25,17},{29,21},{2,10},{... | collective-permute-start | bytes 1769480 | tf_op jit(solution)/shard_map/ppermute | solution.py:861
  285.0 4.0 collective-permute-done.51
  290.9 3.2 collective-permute-done.44
  295.4 9.6 %collective-permute-done.59 = bf16[384,768]{1,0:T(8,128)(2,1)S(1)} collective-permute-done((bf16[384,768]{1,0:T(8,128)(2,1)S(1)}, bf16[384,768]{1,0:T(8,128)(2,1)S(1)}, u32[]{:S(2)}, u32[]{:S(2)}) %collective-permute-start.59) | collective-permute-done | bytes 589856 | tf_op jit(solution)/shard_map/ppermute | solution.py:861
  308.8 3.0 collective-permute-done.55
  313.6 10.7 %collective-permute-start.45 = (bf16[400,768]{1,0:T(8,128)(2,1)S(1)}, bf16[400,768]{1,0:T(8,128)(2,1)S(1)}, u32[]{:S(2)}, u32[]{:S(2)}) collective-permute-start(bf16[400,768]{1,0:T(8,128)(2,1)S(1)} %add_convert_fusion.2), channel_id=1, source_target_pairs={{0,8},{4,12},{24,16},{28,20},{1,9},{5,13},{25,17},{29,21},{2,10},{... | collective-permute-start | bytes 1843208 | tf_op jit(solution)/shard_map/ppermute | solution.py:861
  328.4 11.3 %collective-permute-done.52 = bf16[384,768]{1,0:T(8,128)(2,1)S(1)} collective-permute-done((bf16[384,768]{1,0:T(8,128)(2,1)S(1)}, bf16[384,768]{1,0:T(8,128)(2,1)S(1)}, u32[]{:S(2)}, u32[]{:S(2)}) %collective-permute-start.52) | collective-permute-done | bytes 589856 | tf_op jit(solution)/shard_map/ppermute | solution.py:861
  343.3 7.0 %collective-permute-done.65 = bf16[384,768]{1,0:T(8,128)(2,1)S(1)} collective-permute-done((bf16[384,768]{1,0:T(8,128)(2,1)S(1)}, bf16[384,768]{1,0:T(8,128)(2,1)S(1)}, u32[]{:S(2)}, u32[]{:S(2)}) %collective-permute-start.65) | collective-permute-done | bytes 589856 | tf_op jit(solution)/shard_map/ppermute | solution.py:861
  350.3 5.7 %collective-permute-done.56 = bf16[384,768]{1,0:T(8,128)(2,1)S(1)} collective-permute-done((bf16[384,768]{1,0:T(8,128)(2,1)S(1)}, bf16[384,768]{1,0:T(8,128)(2,1)S(1)}, u32[]{:S(2)}, u32[]{:S(2)}) %collective-permute-start.56) | collective-permute-done | bytes 589856 | tf_op jit(solution)/shard_map/ppermute | solution.py:861
  356.5 9.4 %collective-permute-done.67 = bf16[384,768]{1,0:T(8,128)(2,1)S(1)} collective-permute-done((bf16[384,768]{1,0:T(8,128)(2,1)S(1)}, bf16[384,768]{1,0:T(8,128)(2,1)S(1)}, u32[]{:S(2)}, u32[]{:S(2)}) %collective-permute-start.67) | collective-permute-done | bytes 589856 | tf_op jit(solution)/shard_map/ppermute | solution.py:861
  373.8 4.1 %collective-permute-done.68 = bf16[384,768]{1,0:T(8,128)(2,1)S(1)} collective-permute-done((bf16[384,768]{1,0:T(8,128)(2,1)S(1)}, bf16[384,768]{1,0:T(8,128)(2,1)S(1)}, u32[]{:S(2)}, u32[]{:S(2)}) %collective-permute-start.68) | collective-permute-done | bytes 589856 | tf_op jit(solution)/shard_map/ppermute | solution.py:861
  383.6 6.6 %collective-permute-done.57 = bf16[384,768]{1,0:T(8,128)(2,1)} collective-permute-done((bf16[384,768]{1,0:T(8,128)(2,1)}, bf16[384,768]{1,0:T(8,128)(2,1)}, u32[]{:S(2)}, u32[]{:S(2)}) %collective-permute-start.57) | collective-permute-done | bytes 589856 | tf_op jit(solution)/shard_map/ppermute | solution.py:861
  (532 shorter events, 180.3 us)
Async XLA Ops:
  0.7 23.6 %collective-permute-start = (bf16[3,192,768]{2,1,0:T(8,128)(2,1)}, bf16[3,192,768]{2,1,0:T(8,128)(2,1)S(1)}, u32[]{:S(2)}, u32[]{:S(2)}) collective-permute-start(bf16[3,192,768]{2,1,0:T(8,128)(2,1)} %refs_0_.7), channel_id=1, source_target_pairs={{0,1},{1,0},{2,3},{3,2},{4,5},{5,4},{6,7},{7,6},{8,9},{9,8},{10,11... | collective-permute-start | bytes 2654216 | tf_op jit(solution)/shard_map/ppermute | solution.py:781
  1.2 23.1 %collective-permute-start.1 = (bf16[6,192,768]{2,1,0:T(8,128)(2,1)}, bf16[6,192,768]{2,1,0:T(8,128)(2,1)}, u32[]{:S(2)}, u32[]{:S(2)}) collective-permute-start(bf16[6,192,768]{2,1,0:T(8,128)(2,1)} %refs_1_.7), channel_id=1, source_target_pairs={{0,1},{1,0},{2,3},{3,2},{4,5},{5,4},{6,7},{7,6},{8,9},{9,8},{10,11... | collective-permute-start | bytes 5308424 | tf_op jit(solution)/shard_map/ppermute | solution.py:781
  19.1 22.5 %collective-permute-start.4 = (bf16[3,192,384]{2,1,0:T(8,128)(2,1)}, bf16[3,192,384]{2,1,0:T(8,128)(2,1)}, u32[]{:S(2)}, u32[]{:S(2)}) collective-permute-start(bf16[3,192,384]{2,1,0:T(8,128)(2,1)} %pad_maximum_fusion.7), channel_id=1, source_target_pairs={{0,2},{1,3},{2,0},{3,1},{4,6},{5,7},{6,4},{7,5},{8,10},{9,11},{10,... | collective-permute-start | bytes 1327112 | tf_op jit(solution)/shard_map/ppermute | solution.py:781
  44.8 32.8 %collective-permute-start.9 = (bf16[2,768,768]{2,1,0:T(8,128)(2,1)}, bf16[2,768,768]{2,1,0:T(8,128)(2,1)S(1)}, u32[]{:S(2)}, u32[]{:S(2)}) collective-permute-start(bf16[2,768,768]{2,1,0:T(8,128)(2,1)} %fi.5), channel_id=1, source_target_pairs={{0,1},{1,0},{2,3},{3,2},{4,5},{5,4},{6,7},{7,6},{8,9},{9,8},{10,11... | collective-permute-start | bytes 7077896 | tf_op jit(solution)/shard_map/ppermute | solution.py:781
  44.8 32.8 %collective-permute-start.10 = (bf16[2,768,768]{2,1,0:T(8,128)(2,1)}, bf16[2,768,768]{2,1,0:T(8,128)(2,1)S(1)}, u32[]{:S(2)}, u32[]{:S(2)}) collective-permute-start(bf16[2,768,768]{2,1,0:T(8,128)(2,1)} %fo.5), channel_id=1, source_target_pairs={{0,1},{1,0},{2,3},{3,2},{4,5},{5,4},{6,7},{7,6},{8,9},{9,8},{10,11... | collective-permute-start | bytes 7077896 | tf_op jit(solution)/shard_map/ppermute | solution.py:781
  51.3 26.3 %collective-permute-start.6 = (bf16[3,192,768]{2,1,0:T(8,128)(2,1)}, bf16[3,192,768]{2,1,0:T(8,128)(2,1)S(1)}, u32[]{:S(2)}, u32[]{:S(2)}) collective-permute-start(bf16[3,192,768]{2,1,0:T(8,128)(2,1)} %refs_2_.7), channel_id=1, source_target_pairs={{0,1},{1,0},{2,3},{3,2},{4,5},{5,4},{6,7},{7,6},{8,9},{9,8},{10,11... | collective-permute-start | bytes 2654216 | tf_op jit(solution)/shard_map/ppermute | solution.py:781
  132.4 22.2 %collective-permute-start.24 = (bf16[768,768]{1,0:T(8,128)(2,1)}, bf16[768,768]{1,0:T(8,128)(2,1)S(1)}, u32[]{:S(2)}, u32[]{:S(2)}) collective-permute-start(bf16[768,768]{1,0:T(8,128)(2,1)} %copy-done.66), channel_id=1, source_target_pairs={{0,1},{1,0},{2,3},{3,2},{4,5},{5,4},{6,7},{7,6},{8,9},{9,8},{10,11... | collective-permute-start | bytes 3538952 | tf_op jit(solution)/shard_map/ppermute | solution.py:781
  137.7 33.5 %collective-permute-start.26 = (bf16[384,768]{1,0:T(8,128)(2,1)}, bf16[384,768]{1,0:T(8,128)(2,1)}, u32[]{:S(2)}, u32[]{:S(2)}) collective-permute-start(bf16[384,768]{1,0:T(8,128)(2,1)} %add_convert_fusion.34), channel_id=1, source_target_pairs={{0,4},{4,0},{8,12},{12,8},{16,20},{20,16},{24,28},{28,24},{1,5},{5... | collective-permute-start | bytes 1769480 | tf_op jit(solution)/shard_map/ppermute | solution.py:861
  167.3 25.5 %collective-permute-start.28 = (bf16[4,192,768]{2,1,0:T(8,128)(2,1)}, bf16[4,192,768]{2,1,0:T(8,128)(2,1)}, u32[]{:S(2)}, u32[]{:S(2)}) collective-permute-start(bf16[4,192,768]{2,1,0:T(8,128)(2,1)} %get-tuple-element.233), channel_id=1, source_target_pairs={{0,1},{1,0},{2,3},{3,2},{4,5},{5,4},{6,7},{7,6},{8,9},{9,8},{10,11... | collective-permute-start | bytes 3538952 | tf_op jit(solution)/shard_map/ppermute | solution.py:781
  170.6 24.8 %collective-permute-start.25 = (bf16[512,768]{1,0:T(8,128)(2,1)}, bf16[512,768]{1,0:T(8,128)(2,1)}, u32[]{:S(2)}, u32[]{:S(2)}) collective-permute-start(bf16[512,768]{1,0:T(8,128)(2,1)} %copy-done.69), channel_id=1, source_target_pairs={{0,2},{1,3},{2,0},{3,1},{4,6},{5,7},{6,4},{7,5},{8,10},{9,11},{10,... | collective-permute-start | bytes 2359304 | tf_op jit(solution)/shard_map/ppermute | solution.py:781
  175.0 28.6 %collective-permute-start.30 = (bf16[384,768]{1,0:T(8,128)(2,1)}, bf16[384,768]{1,0:T(8,128)(2,1)}, u32[]{:S(2)}, u32[]{:S(2)}) collective-permute-start(bf16[384,768]{1,0:T(8,128)(2,1)} %get-tuple-element.220), channel_id=1, source_target_pairs={{0,8},{4,12},{24,16},{28,20},{1,9},{5,13},{25,17},{29,21},{2,10},{... | collective-permute-start | bytes 1769480 | tf_op jit(solution)/shard_map/ppermute | solution.py:861
  187.0 20.8 %collective-permute-start.29 = (bf16[4,192,768]{2,1,0:T(8,128)(2,1)}, bf16[4,192,768]{2,1,0:T(8,128)(2,1)}, u32[]{:S(2)}, u32[]{:S(2)}) collective-permute-start(bf16[4,192,768]{2,1,0:T(8,128)(2,1)} %get-tuple-element.239), channel_id=1, source_target_pairs={{0,1},{1,0},{2,3},{3,2},{4,5},{5,4},{6,7},{7,6},{8,9},{9,8},{10,11... | collective-permute-start | bytes 3538952 | tf_op jit(solution)/shard_map/ppermute | solution.py:781
  194.1 28.3 %collective-permute-start.32 = (bf16[384,768]{1,0:T(8,128)(2,1)S(1)}, bf16[384,768]{1,0:T(8,128)(2,1)S(1)}, u32[]{:S(2)}, u32[]{:S(2)}) collective-permute-start(bf16[384,768]{1,0:T(8,128)(2,1)S(1)} %add_convert_fusion.28), channel_id=1, source_target_pairs={{0,4},{4,0},{8,12},{12,8},{16,20},{20,16},{24,28},{28,24},{1,5},{5... | collective-permute-start | bytes 1769480 | tf_op jit(solution)/shard_map/ppermute | solution.py:861
  205.5 25.9 %collective-permute-start.31 = (bf16[768,768]{1,0:T(8,128)(2,1)S(1)}, bf16[768,768]{1,0:T(8,128)(2,1)S(1)}, u32[]{:S(2)}, u32[]{:S(2)}) collective-permute-start(bf16[768,768]{1,0:T(8,128)(2,1)S(1)} %get-tuple-element.248), channel_id=1, source_target_pairs={{0,1},{1,0},{2,3},{3,2},{4,5},{5,4},{6,7},{7,6},{8,9},{9,8},{10,11... | collective-permute-start | bytes 3538952 | tf_op jit(solution)/shard_map/ppermute | solution.py:781
  205.6 24.0 %collective-permute-start.46 = (bf16[384,768]{1,0:T(8,128)(2,1)S(1)}, bf16[384,768]{1,0:T(8,128)(2,1)S(1)}, u32[]{:S(2)}, u32[]{:S(2)}) collective-permute-start(bf16[384,768]{1,0:T(8,128)(2,1)S(1)} %add_convert_fusion.26), channel_id=1, source_target_pairs={{8,16},{12,20},{16,8},{20,12},{9,17},{13,21},{17,9},{21,13},{10,18... | collective-permute-start | bytes 1769480 | tf_op jit(solution)/shard_map/ppermute | solution.py:861
  206.4 37.3 %collective-permute-start.40 = (bf16[768,768]{1,0:T(8,128)(2,1)S(1)}, bf16[768,768]{1,0:T(8,128)(2,1)S(1)}, u32[]{:S(2)}, u32[]{:S(2)}) collective-permute-start(bf16[768,768]{1,0:T(8,128)(2,1)S(1)} %get-tuple-element.270), channel_id=1, source_target_pairs={{0,1},{1,0},{2,3},{3,2},{4,5},{5,4},{6,7},{7,6},{8,9},{9,8},{10,11... | collective-permute-start | bytes 3538952 | tf_op jit(solution)/shard_map/ppermute | solution.py:781
  210.0 42.0 %collective-permute-start.41 = (bf16[384,768]{1,0:T(8,128)(2,1)}, bf16[384,768]{1,0:T(8,128)(2,1)}, u32[]{:S(2)}, u32[]{:S(2)}) collective-permute-start(bf16[384,768]{1,0:T(8,128)(2,1)} %add_convert_fusion.27), channel_id=1, source_target_pairs={{0,4},{4,0},{8,12},{12,8},{16,20},{20,16},{24,28},{28,24},{1,5},{5... | collective-permute-start | bytes 1769480 | tf_op jit(solution)/shard_map/ppermute | solution.py:861
  224.6 22.6 %collective-permute-start.43 = (bf16[384,768]{1,0:T(8,128)(2,1)}, bf16[384,768]{1,0:T(8,128)(2,1)}, u32[]{:S(2)}, u32[]{:S(2)}) collective-permute-start(bf16[384,768]{1,0:T(8,128)(2,1)} %add_convert_fusion.17), channel_id=1, source_target_pairs={{0,8},{4,12},{24,16},{28,20},{1,9},{5,13},{25,17},{29,21},{2,10},{... | collective-permute-start | bytes 1769480 | tf_op jit(solution)/shard_map/ppermute | solution.py:861
  229.8 20.8 %collective-permute-start.50 = (bf16[384,768]{1,0:T(8,128)(2,1)S(1)}, bf16[384,768]{1,0:T(8,128)(2,1)}, u32[]{:S(2)}, u32[]{:S(2)}) collective-permute-start(bf16[384,768]{1,0:T(8,128)(2,1)S(1)} %add_convert_fusion.12), channel_id=1, source_target_pairs={{8,0},{12,4},{16,24},{20,28},{9,1},{13,5},{17,25},{21,29},{10,2},{... | collective-permute-start | bytes 1769480 | tf_op jit(solution)/shard_map/ppermute | solution.py:861
  250.6 29.8 %collective-permute-start.36 = (bf16[4,192,768]{2,1,0:T(8,128)(2,1)S(1)}, bf16[4,192,768]{2,1,0:T(8,128)(2,1)S(1)}, u32[]{:S(2)}, u32[]{:S(2)}) collective-permute-start(bf16[4,192,768]{2,1,0:T(8,128)(2,1)S(1)} %copy-done.68), channel_id=1, source_target_pairs={{0,1},{1,0},{2,3},{3,2},{4,5},{5,4},{6,7},{7,6},{8,9},{9,8},{10,11... | collective-permute-start | bytes 3538952 | tf_op jit(solution)/shard_map/ppermute | solution.py:781
  255.4 20.9 %collective-permute-start.63 = (bf16[384,768]{1,0:T(8,128)(2,1)S(1)}, bf16[384,768]{1,0:T(8,128)(2,1)S(1)}, u32[]{:S(2)}, u32[]{:S(2)}) collective-permute-start(bf16[384,768]{1,0:T(8,128)(2,1)S(1)} %add_convert_fusion.3), channel_id=1, source_target_pairs={{8,0},{12,4},{16,24},{20,28},{9,1},{13,5},{17,25},{21,29},{10,2},{... | collective-permute-start | bytes 1769480 | tf_op jit(solution)/shard_map/ppermute | solution.py:861
  261.7 20.5 %collective-permute-start.58 = (bf16[384,768]{1,0:T(8,128)(2,1)S(1)}, bf16[384,768]{1,0:T(8,128)(2,1)S(1)}, u32[]{:S(2)}, u32[]{:S(2)}) collective-permute-start(bf16[384,768]{1,0:T(8,128)(2,1)S(1)} %add_convert_fusion.8), channel_id=1, source_target_pairs={{0,8},{4,12},{24,16},{28,20},{1,9},{5,13},{25,17},{29,21},{2,10},{... | collective-permute-start | bytes 1769480 | tf_op jit(solution)/shard_map/ppermute | solution.py:861
  280.8 31.3 %collective-permute-start.39 = (bf16[400,768]{1,0:T(8,128)(2,1)S(1)}, bf16[400,768]{1,0:T(8,128)(2,1)S(1)}, u32[]{:S(2)}, u32[]{:S(2)}) collective-permute-start(bf16[400,768]{1,0:T(8,128)(2,1)S(1)} %pad_maximum_fusion.5), channel_id=1, source_target_pairs={{0,4},{4,0},{8,12},{12,8},{16,20},{20,16},{24,28},{28,24},{1,5},{5... | collective-permute-start | bytes 1843208 | tf_op jit(solution)/shard_map/ppermute | solution.py:861
  282.1 22.9 %collective-permute-start.59 = (bf16[384,768]{1,0:T(8,128)(2,1)S(1)}, bf16[384,768]{1,0:T(8,128)(2,1)S(1)}, u32[]{:S(2)}, u32[]{:S(2)}) collective-permute-start(bf16[384,768]{1,0:T(8,128)(2,1)S(1)} %add_convert_fusion.10), channel_id=1, source_target_pairs={{0,8},{4,12},{24,16},{28,20},{1,9},{5,13},{25,17},{29,21},{2,10},{... | collective-permute-start | bytes 1769480 | tf_op jit(solution)/shard_map/ppermute | solution.py:861
  289.7 22.1 %collective-permute-start.55 = (bf16[384,768]{1,0:T(8,128)(2,1)S(1)}, bf16[384,768]{1,0:T(8,128)(2,1)S(1)}, u32[]{:S(2)}, u32[]{:S(2)}) collective-permute-start(bf16[384,768]{1,0:T(8,128)(2,1)S(1)} %broadcast_select_fusion.5), channel_id=1, source_target_pairs={{0,4},{4,0},{8,12},{12,8},{16,20},{20,16},{24,28},{28,24},{1,5},{5... | collective-permute-start | bytes 1769480 | tf_op jit(solution)/shard_map/ppermute | solution.py:861
  306.1 21.0 %collective-permute-start.64 = (bf16[384,768]{1,0:T(8,128)(2,1)S(1)}, bf16[384,768]{1,0:T(8,128)(2,1)S(1)}, u32[]{:S(2)}, u32[]{:S(2)}) collective-permute-start(bf16[384,768]{1,0:T(8,128)(2,1)S(1)} %add_convert_fusion.4), channel_id=1, source_target_pairs={{8,0},{12,4},{16,24},{20,28},{9,1},{13,5},{17,25},{21,29},{10,2},{... | collective-permute-start | bytes 1769480 | tf_op jit(solution)/shard_map/ppermute | solution.py:861
  307.5 32.1 %collective-permute-start.52 = (bf16[384,768]{1,0:T(8,128)(2,1)S(1)}, bf16[384,768]{1,0:T(8,128)(2,1)S(1)}, u32[]{:S(2)}, u32[]{:S(2)}) collective-permute-start(bf16[384,768]{1,0:T(8,128)(2,1)S(1)} %add_convert_fusion.14), channel_id=1, source_target_pairs={{8,0},{12,4},{16,24},{20,28},{9,1},{13,5},{17,25},{21,29},{10,2},{... | collective-permute-start | bytes 1769480 | tf_op jit(solution)/shard_map/ppermute | solution.py:861
  312.1 28.6 %collective-permute-start.66 = (bf16[384,768]{1,0:T(8,128)(2,1)S(1)}, bf16[384,768]{1,0:T(8,128)(2,1)S(1)}, u32[]{:S(2)}, u32[]{:S(2)}) collective-permute-start(bf16[384,768]{1,0:T(8,128)(2,1)S(1)} %broadcast_select_fusion.1), channel_id=1, source_target_pairs={{0,4},{4,0},{8,12},{12,8},{16,20},{20,16},{24,28},{28,24},{1,5},{5... | collective-permute-start | bytes 1769480 | tf_op jit(solution)/shard_map/ppermute | solution.py:861
  313.6 28.3 %collective-permute-start.45 = (bf16[400,768]{1,0:T(8,128)(2,1)S(1)}, bf16[400,768]{1,0:T(8,128)(2,1)S(1)}, u32[]{:S(2)}, u32[]{:S(2)}) collective-permute-start(bf16[400,768]{1,0:T(8,128)(2,1)S(1)} %add_convert_fusion.2), channel_id=1, source_target_pairs={{0,8},{4,12},{24,16},{28,20},{1,9},{5,13},{25,17},{29,21},{2,10},{... | collective-permute-start | bytes 1843208 | tf_op jit(solution)/shard_map/ppermute | solution.py:861
  327.0 23.2 %collective-permute-start.65 = (bf16[384,768]{1,0:T(8,128)(2,1)S(1)}, bf16[384,768]{1,0:T(8,128)(2,1)S(1)}, u32[]{:S(2)}, u32[]{:S(2)}) collective-permute-start(bf16[384,768]{1,0:T(8,128)(2,1)S(1)} %add_convert_fusion.5), channel_id=1, source_target_pairs={{8,0},{12,4},{16,24},{20,28},{9,1},{13,5},{17,25},{21,29},{10,2},{... | collective-permute-start | bytes 1769480 | tf_op jit(solution)/shard_map/ppermute | solution.py:861
  340.8 25.2 %collective-permute-start.67 = (bf16[384,768]{1,0:T(8,128)(2,1)S(1)}, bf16[384,768]{1,0:T(8,128)(2,1)S(1)}, u32[]{:S(2)}, u32[]{:S(2)}) collective-permute-start(bf16[384,768]{1,0:T(8,128)(2,1)S(1)} %broadcast_select_fusion.2), channel_id=1, source_target_pairs={{0,4},{4,0},{8,12},{12,8},{16,20},{20,16},{24,28},{28,24},{1,5},{5... | collective-permute-start | bytes 1769480 | tf_op jit(solution)/shard_map/ppermute | solution.py:861
  342.0 24.9 %collective-permute-start.49 = (bf16[400,768]{1,0:T(8,128)(2,1)S(1)}, bf16[400,768]{1,0:T(8,128)(2,1)S(1)}, u32[]{:S(2)}, u32[]{:S(2)}) collective-permute-start(bf16[400,768]{1,0:T(8,128)(2,1)S(1)} %add_convert_fusion.1), channel_id=1, source_target_pairs={{8,16},{12,20},{16,8},{20,12},{9,17},{13,21},{17,9},{21,13},{10,18... | collective-permute-start | bytes 1843208 | tf_op jit(solution)/shard_map/ppermute | solution.py:861
  (191 other events, 1472.7 us)
where the time goes:
time: 404 us; the launch traced here: 400 us
  waiting for transfers between devices  105 us (26%)
  Pallas kernels  92.6 us (23%)
  starting transfers between devices  84.4 us (21%)
  other arithmetic  54.1 us (13%)
  local copies, waits for them, and re-layouts  54 us (13%)
  between operations  7.56 us (2%)
    pallas_call x13, Pallas kernels, call(): pl.pallas_call(kernel, grid_spec=pltpu.PrefetchScalarGridSpec(num_scalar_...  92.6 us
    ppermute x35, waiting for transfers between devices, step(): got = lax.ppermute(sent, 'dp', ROUTES[link])  74.5 us
    ppermute x35, starting transfers between devices, step(): got = lax.ppermute(sent, 'dp', ROUTES[link])  65.3 us
    unnamed x309, local copies, waits for them, and re-layouts  40.6 us
    convert_element_type x27, other arithmetic, add_low(): return (a.astype(f32) + b.astype(f32)).astype(bf16)  25.2 us
    ppermute x30, waiting for transfers between devices, swap_section(): return lax.ppermute(value, 'section', [(i, i ^ bit) for i in range(count)])  23 us
    ppermute x30, starting transfers between devices, swap_section(): return lax.ppermute(value, 'section', [(i, i ^ bit) for i in range(count)])  14.2 us
  transfers between devices with their start and end apart: 69, of which 24 were waited for; matrix products, arithmetic and copies ran while one was open for 15% of the time, Pallas kernels for 20%

commit v1 on v0

--- a/solution.py
+++ b/solution.py
@@ -880,12 +880,9 @@
         free = {name: 0.0 for name in ROUTES}
         at = {i: late.get(i, 0.0) for i in self.stage}
         while min(self.stage.values()) < len(STAGES):
-            best = None
-            for i, now in self.stage.items():
-                if now < len(STAGES):
-                    key = (max(at[i], free[STAGES[now][0]]), now - len(STAGES), i)
-                    best = key if best is None else min(best, key)
-            begin, _, i = best
+            choices = [(max(at[i], free[STAGES[now][0]]), now, i) for i, now in self.stage.items() if now < len(STAGES)]
+            soon = min(choices)[0] + 6.0
+            begin, _, i = min((c for c in choices if c[0] <= soon), key=lambda c: (c[1], c[0]))
             link, length = STAGES[self.stage[i]]
             free[link], at[i] = begin + length + 0.5, begin + length + STEP
             self.step(i)
@@ -1023,7 +1020,7 @@
     small = jnp.concatenate([gain0, gain1, gain2, gains34, tables, jnp.zeros((10, D), f32)])
     small = small + swap_section(small, 1)
     sums.enter(6, own_enc, got_w, small.astype(bf16))
-    total = sums.finish({6: 6.0})
+    total = sums.finish({0: 0.0, 2: 0.0, 5: 4.0, 3: 14.0, 4: 4.0, 6: 10.0})
     unit_out2, unit_in2, unit_cross, unit_out1, unit_in1, unit_self, unit_enc = (total[i] for i in range(7))
     small = sums.extra.astype(f32)
     gains = small[:5]
@@ -1046,9 +1043,15 @@
     u_enc, u_self, u_cross = (
         u.reshape(4, quarter, D).astype(f32) for u in (unit_enc, unit_self, unit_cross)
     )
-    query_grad = jnp.stack([u_enc[0], u_self[0], u_cross[0]])
-    keyval_grad = jnp.concatenate([u_enc[1:3], u_self[1:3], u_cross[1:3]])
-    output_grad = jnp.stack([u_enc[3], u_self[3], u_cross[3]])
+    def placed(count, parts):
+        whole_grad = jnp.zeros((count, quarter, D), f32)
+        for at, part in parts:
+            whole_grad = lax.dynamic_update_slice_in_dim(whole_grad, part, at, 0)
+        return whole_grad
+
+    query_grad = placed(3, ((2, u_cross[0:1]), (1, u_self[0:1]), (0, u_enc[0:1])))
+    keyval_grad = placed(6, ((4, u_cross[1:3]), (2, u_self[1:3]), (0, u_enc[1:3])))
+    output_grad = placed(3, ((2, u_cross[3:4]), (1, u_self[3:4]), (0, u_enc[3:4])))
     feed_in_grad = jnp.stack([unit_in1, unit_in2]).astype(f32)
     feed_out_grad = jnp.stack([unit_out1, unit_out2]).astype(f32)
     return (

time: 404 us -> 401 us (level)
  other arithmetic: 54.1 us -> 49.5 us
    unnamed x309 -> x307, local copies, waits for them, and re-layouts: 40.6 us -> 41.6 us
  transfers between devices with their start and end apart: 69 -> 69, of which waited for: 24 -> 22; matrix products, arithmetic and copies ran while one was open for 15% -> 16% of each run, Pallas kernels for 20% -> 20%
where the time goes in v1:
time: 401 us; the launch traced here: 397 us
  waiting for transfers between devices  103 us (26%)
  Pallas kernels  92.6 us (23%)
  starting transfers between devices  85.7 us (21%)
  local copies, waits for them, and re-layouts  56.3 us (14%)
  other arithmetic  49.5 us (12%)
  between operations  7.68 us (2%)
    pallas_call x13, Pallas kernels, call(): pl.pallas_call(kernel, grid_spec=pltpu.PrefetchScalarGridSpec(num_scalar_...  92.6 us
    ppermute x35, waiting for transfers between devices, step(): got = lax.ppermute(sent, 'dp', ROUTES[link])  72 us
    ppermute x35, starting transfers between devices, step(): got = lax.ppermute(sent, 'dp', ROUTES[link])  66.7 us
    unnamed x307, local copies, waits for them, and re-layouts  41.6 us
    convert_element_type x27, other arithmetic, add_low(): return (a.astype(f32) + b.astype(f32)).astype(bf16)  25.2 us
    ppermute x30, waiting for transfers between devices, swap_section(): return lax.ppermute(value, 'section', [(i, i ^ bit) for i in range(count)])  23.1 us
    ppermute x30, starting transfers between devices, swap_section(): return lax.ppermute(value, 'section', [(i, i ^ bit) for i in range(count)])  14.2 us
  transfers between devices with their start and end apart: 69, of which 22 were waited for; matrix products, arithmetic and copies ran while one was open for 16% of the time, Pallas kernels for 20%

profile of v1, /device:TPU:0, one launch (start us, length us, event | category | flops | bytes accessed | tf_op | source)
XLA Modules:
  0.0 396.6 jit_solution(9694525959390707677)
XLA Ops:
  4.7 3.0 collective-permute-start.2
  7.8 2.8 multiply_reduce_fusion
  26.1 8.7 %shard_map.240 = (bf16[3,512,384]{2,1,0:T(8,128)(2,1)S(1)}, bf16[512,384]{1,0:T(8,128)(2,1)S(1)}, bf16[6,384,384]{2,1,0:T(8,128)(2,1)S(1)}, bf16[6,128,128]{2,1,...) custom-call(s32[18]{0:T(128)S(1)} %concatenate.151.at, ...), custom_call_target="tpu_custom_call" | custom-call | flops 20000000000 | bytes 1048576 | tf_op jit(solution)/shard_map/pallas_call | solution.py:121
  46.4 4.8 %collective-permute-done.7.go = bf16[192,768]{1,0:T(8,128)(2,1)} collective-permute-done((bf16[192,768]{1,0:T(8,128)(2,1)}, bf16[192,768]{1,0:T(8,128)(2,1)}, u32[]{:S(2)}, u32[]{:S(2)}) %collective-permute-start.7) | collective-permute-done | bytes 294944 | tf_op jit(solution)/shard_map/ppermute | solution.py:781
  54.9 8.6 %shard_map.241 = (bf16[3,512,384]{2,1,0:T(8,128)(2,1)S(1)}, bf16[512,384]{1,0:T(8,128)(2,1)S(1)}, bf16[6,384,384]{2,1,0:T(8,128)(2,1)S(1)}, bf16[6,128,128]{2,1,0:T(8,128)(2,1)S(1)}, bf16[3,768,384]{2,1,0:T(8,128)(2,1)S(1)}) custom-call(s32[18]{0:T(128)S(1)} %concatenate.151.at, bf16[512,768]{1,0:T(8,128)(2,1)S(1)} %copy-done.115, f32[5,768]{1,0:T(8,128)S(1)} %copy-done.44, ...), custom_call_target="tpu_custom_call" | custom-call | flops 20000000000 | bytes 1048576 | tf_op jit(solution)/shard_map/pallas_call | solution.py:121
  68.7 6.0 %collective-permute-done.15 = bf16[4,48,768]{2,1,0:T(8,128)(2,1)S(1)} collective-permute-done((bf16[4,48,768]{2,1,0:T(8,128)(2,1)}, bf16[4,48,768]{2,1,0:T(8,128)(2,1)S(1)}, u32[]{:S(2)}, u32[]{:S(2)}) %collective-permute-start.15) | collective-permute-done | bytes 294944 | tf_op jit(solution)/shard_map/ppermute | solution.py:786
  78.1 9.4 %shard_map.242 = (bf16[512,768]{1,0:T(8,128)(2,1)S(1)}, bf16[512,768]{1,0:T(8,128)(2,1)S(1)}, bf16[512,1536]{1,0:T(8,128)(2,1)S(1)}, bf16[512,1536]{1,0:T(8,128)...) custom-call(s32[18]{0:T(128)S(1)} %concatenate.151.at, bf16[512,768]{1,0:T(8,128)(2,1)S(1)} %copy-done.112, ...), custom_call_target="tpu_custom_call" | custom-call | flops 20000000000 | bytes 1048576 | tf_op jit(solution)/shard_map/pallas_call | solution.py:121
  92.8 4.2 %shard_map.243 = (bf16[96,768]{1,0:T(8,128)(2,1)S(1)}, bf16[96,768]{1,0:T(8,128)(2,1)S(1)}, bf16[96,768]{1,0:T(8,128)(2,1)S(1)}, bf16[96,768]{1,0:T(8,128)(2,1)S...) custom-call(s32[18]{0:T(128)S(1)} %concatenate.151.at, ...), custom_call_target="tpu_custom_call" | custom-call | flops 100000000 | bytes 1048576 | tf_op jit(solution)/shard_map/pallas_call | solution.py:121
  101.0 10.2 %collective-permute-done.11.p1 = bf16[512,768]{1,0:T(8,128)(2,1)S(1)} collective-permute-done((bf16[512,768]{1,0:T(8,128)(2,1)S(1)}, bf16[512,768]{1,0:T(8,128)(2,1)S(1)}, u32[]{:S(2)}, u32[]{:S(2)}) %collective-permute-start.11) | collective-permute-done | bytes 786464 | tf_op jit(solution)/shard_map/ppermute | solution.py:781
  111.2 9.6 %shard_map.244 = (bf16[512,768]{1,0:T(8,128)(2,1)S(1)}, bf16[96,768]{1,0:T(8,128)(2,1)S(1)}, bf16[512,768]{1,0:T(8,128)(2,1)S(1)}, bf16[512,768]{1,0:T(8,128)(2,...) custom-call(s32[18]{0:T(128)S(1)} %concatenate.151.at, ...), custom_call_target="tpu_custom_call" | custom-call | flops 20000000000 | bytes 1048576 | tf_op jit(solution)/shard_map/pallas_call | solution.py:121
  120.9 3.7 shard_map.245
  147.7 6.8 %shard_map.246 = (bf16[96,768]{1,0:T(8,128)(2,1)S(1)}, bf16[96,768]{1,0:T(8,128)(2,1)S(1)}, bf16[512,768]{1,0:T(8,128)(2,1)S(1)}, bf16[512,768]{1,0:T(8,128)(2,1...) custom-call(s32[18]{0:T(128)S(1)} %concatenate.151.at, ...), custom_call_target="tpu_custom_call" | custom-call | flops 20000000000 | bytes 1048576 | tf_op jit(solution)/shard_map/pallas_call | solution.py:121
  157.2 6.3 %shard_map.247 = (bf16[512,1536]{1,0:T(8,128)(2,1)S(1)}, bf16[512,768]{1,0:T(8,128)(2,1)S(1)}) custom-call(s32[18]{0:T(128)S(1)} %concatenate.151.at, bf16[512,768]{1,0:T(8,128)(2,1)S(1)} %get-tuple-element.206.de_ref.refs_1_.refs_3_, bf16[512,1536]{1,0:T(8,128)(2,1)S(1)} %copy-done.98, bf16[2,768,768]{2,1,0:T(8,128)(2,1)S(1)} %copy-done.56, ...), custom_call_target="tpu_custom_call" | custom-call | flops 20000000000 | bytes 1048576 | tf_op jit(solution)/shard_map/pallas_call | solution.py:121
  171.2 3.8 add_convert_fusion.29
  175.0 3.2 collective-permute-start.30
  178.3 7.1 %shard_map.249 = (bf16[4,192,768]{2,1,0:T(8,128)(2,1)S(1)}, bf16[4,192,768]{2,1,0:T(8,128)(2,1)}, bf16[96,768]{1,0:T(8,128)(2,1)S(1)}, f32[1,768]{1,0:T(1,128)S(1)}, f32[3,32,128]{2,1,0:T(8,128)S(1)}) custom-call(s32[18]{0:T(128)S(1)} %concatenate.151.at, f32[96,768]{1,0:T(8,128)S(1)} %get-tuple-element.221.dm_ref, f32[5,768]{1,0:T(8,128)S(1)} %copy-done.46, ...), custom_call_target="tpu_custom_call" | custom-call | flops 1000000000 | bytes 1048576 | tf_op jit(solution)/shard_map/pallas_call | solution.py:121
  199.4 4.2 %shard_map.250 = (bf16[768,768]{1,0:T(8,128)(2,1)S(1)}, bf16[768,768]{1,0:T(8,128)(2,1)S(1)}, bf16[768,768]{1,0:T(8,128)(2,1)S(1)}, bf16[768,768]{1,0:T(8,128)(2,1)S(1)}) custom-call(s32[18]{0:T(128)S(1)} %concatenate.151.at, bf16[512,1536]{1,0:T(8,128)(2,1)S(1)} %copy-done.79, bf16[512,768]{1,0:T(8,128)(2,1)S(1)} %copy-done.85, ...), custom_call_target="tpu_custom_call" | custom-call | flops 10000000000 | bytes 1048576 | tf_op jit(solution)/shard_map/pallas_call | solution.py:121
  210.9 11.4 %shard_map.251 = (bf16[4,192,768]{2,1,0:T(8,128)(2,1)S(1)}, bf16[4,192,768]{2,1,0:T(8,128)(2,1)S(1)}, f32[6,3,512]{2,1,0:T(4,128)S(1)}, f32[6,1,256]{2,1,0:T(1,1...) custom-call(s32[18]{0:T(128)S(1)} %concatenate.151.at, ...), custom_call_target="tpu_custom_call" | custom-call | flops 20000000000 | bytes 1048576 | tf_op jit(solution)/shard_map/pallas_call | solution.py:121
  224.6 5.0 %collective-permute-start.36 = (bf16[384,768]{1,0:T(8,128)(2,1)}, bf16[384,768]{1,0:T(8,128)(2,1)}, u32[]{:S(2)}, u32[]{:S(2)}) collective-permute-start(bf16[384,768]{1,0:T(8,128)(2,1)} %add_convert_fusion.22), channel_id=1, source_target_pairs={{0,8},{4,12},{24,16},{28,20},{1,9},{5,13},{25,17},{29,21},{2,10},{... | collective-permute-start | bytes 1769480 | tf_op jit(solution)/shard_map/ppermute | solution.py:861
  234.0 9.8 %shard_map.252 = (bf16[4,192,768]{2,1,0:T(8,128)(2,1)S(1)}, bf16[4,192,768]{2,1,0:T(8,128)(2,1)S(1)}, f32[6,3,512]{2,1,0:T(4,128)S(1)}, f32[6,1,256]{2,1,0:T(1,1...) custom-call(s32[18]{0:T(128)S(1)} %concatenate.151.at, ...), custom_call_target="tpu_custom_call", output_to_operand_aliasing={{0}: (15, {}), {1}: (16, {})} | custom-call | flops 20000000000 | bytes 1048576 | tf_op jit(solution)/shard_map/pallas_call | solution.py:121
  255.3 8.0 %collective-permute-start.46 = (bf16[384,768]{1,0:T(8,128)(2,1)S(1)}, bf16[384,768]{1,0:T(8,128)(2,1)S(1)}, u32[]{:S(2)}, u32[]{:S(2)}) collective-permute-start(bf16[384,768]{1,0:T(8,128)(2,1)S(1)} %add_convert_fusion.16), channel_id=1, source_target_pairs={{0,8},{4,12},{24,16},{28,20},{1,9},{5,13},{25,17},{29,21},{2,10},{... | collective-permute-start | bytes 1769480 | tf_op jit(solution)/shard_map/ppermute | solution.py:861
  266.8 9.4 %collective-permute-start.57 = (bf16[384,768]{1,0:T(8,128)(2,1)S(1)}, bf16[384,768]{1,0:T(8,128)(2,1)S(1)}, u32[]{:S(2)}, u32[]{:S(2)}) collective-permute-start(bf16[384,768]{1,0:T(8,128)(2,1)S(1)} %add_convert_fusion.9), channel_id=1, source_target_pairs={{0,8},{4,12},{24,16},{28,20},{1,9},{5,13},{25,17},{29,21},{2,10},{... | collective-permute-start | bytes 1769480 | tf_op jit(solution)/shard_map/ppermute | solution.py:861
  279.1 2.8 collective-permute-done.49
  283.0 5.5 %collective-permute-start.65 = (bf16[384,768]{1,0:T(8,128)(2,1)S(1)}, bf16[384,768]{1,0:T(8,128)(2,1)S(1)}, u32[]{:S(2)}, u32[]{:S(2)}) collective-permute-start(bf16[384,768]{1,0:T(8,128)(2,1)S(1)} %add_convert_fusion.5), channel_id=1, source_target_pairs={{0,8},{4,12},{24,16},{28,20},{1,9},{5,13},{25,17},{29,21},{2,10},{... | collective-permute-start | bytes 1769480 | tf_op jit(solution)/shard_map/ppermute | solution.py:861
  295.5 5.9 %collective-permute-done.65 = bf16[384,768]{1,0:T(8,128)(2,1)S(1)} collective-permute-done((bf16[384,768]{1,0:T(8,128)(2,1)S(1)}, bf16[384,768]{1,0:T(8,128)(2,1)S(1)}, u32[]{:S(2)}, u32[]{:S(2)}) %collective-permute-start.65) | collective-permute-done | bytes 589856 | tf_op jit(solution)/shard_map/ppermute | solution.py:861
  305.9 17.6 %collective-permute-done.50 = bf16[384,768]{1,0:T(8,128)(2,1)S(1)} collective-permute-done((bf16[384,768]{1,0:T(8,128)(2,1)S(1)}, bf16[384,768]{1,0:T(8,128)(2,1)S(1)}, u32[]{:S(2)}, u32[]{:S(2)}) %collective-permute-start.50) | collective-permute-done | bytes 589856 | tf_op jit(solution)/shard_map/ppermute | solution.py:861
  324.9 4.6 %collective-permute-start.58 = (bf16[400,768]{1,0:T(8,128)(2,1)S(1)}, bf16[400,768]{1,0:T(8,128)(2,1)S(1)}, u32[]{:S(2)}, u32[]{:S(2)}) collective-permute-start(bf16[400,768]{1,0:T(8,128)(2,1)S(1)} %add_convert_fusion.2), channel_id=1, source_target_pairs={{0,8},{4,12},{24,16},{28,20},{1,9},{5,13},{25,17},{29,21},{2,10},{... | collective-permute-start | bytes 1843208 | tf_op jit(solution)/shard_map/ppermute | solution.py:861
  330.8 5.3 %collective-permute-done.61 = bf16[384,768]{1,0:T(8,128)(2,1)S(1)} collective-permute-done((bf16[384,768]{1,0:T(8,128)(2,1)S(1)}, bf16[384,768]{1,0:T(8,128)(2,1)S(1)}, u32[]{:S(2)}, u32[]{:S(2)}) %collective-permute-start.61) | collective-permute-done | bytes 589856 | tf_op jit(solution)/shard_map/ppermute | solution.py:861
  341.3 5.4 %collective-permute-done.67 = bf16[384,768]{1,0:T(8,128)(2,1)S(1)} collective-permute-done((bf16[384,768]{1,0:T(8,128)(2,1)S(1)}, bf16[384,768]{1,0:T(8,128)(2,1)S(1)}, u32[]{:S(2)}, u32[]{:S(2)}) %collective-permute-start.67) | collective-permute-done | bytes 589856 | tf_op jit(solution)/shard_map/ppermute | solution.py:861
  348.2 10.6 %collective-permute-done.63 = bf16[384,768]{1,0:T(8,128)(2,1)S(1)} collective-permute-done((bf16[384,768]{1,0:T(8,128)(2,1)S(1)}, bf16[384,768]{1,0:T(8,128)(2,1)S(1)}, u32[]{:S(2)}, u32[]{:S(2)}) %collective-permute-start.63) | collective-permute-done | bytes 589856 | tf_op jit(solution)/shard_map/ppermute | solution.py:861
  363.3 5.0 %collective-permute-done.56 = bf16[384,768]{1,0:T(8,128)(2,1)S(1)} collective-permute-done((bf16[384,768]{1,0:T(8,128)(2,1)S(1)}, bf16[384,768]{1,0:T(8,128)(2,1)S(1)}, u32[]{:S(2)}, u32[]{:S(2)}) %collective-permute-start.56) | collective-permute-done | bytes 589856 | tf_op jit(solution)/shard_map/ppermute | solution.py:861
  373.4 11.6 %collective-permute-done.68 = bf16[384,768]{1,0:T(8,128)(2,1)S(1)} collective-permute-done((bf16[384,768]{1,0:T(8,128)(2,1)S(1)}, bf16[384,768]{1,0:T(8,128)(2,1)S(1)}, u32[]{:S(2)}, u32[]{:S(2)}) %collective-permute-start.68) | collective-permute-done | bytes 589856 | tf_op jit(solution)/shard_map/ppermute | solution.py:861
  (530 shorter events, 168.6 us)
Async XLA Ops:
  0.7 23.6 %collective-permute-start = (bf16[3,192,768]{2,1,0:T(8,128)(2,1)}, bf16[3,192,768]{2,1,0:T(8,128)(2,1)S(1)}, u32[]{:S(2)}, u32[]{:S(2)}) collective-permute-start(bf16[3,192,768]{2,1,0:T(8,128)(2,1)} %refs_0_.7), channel_id=1, source_target_pairs={{0,1},{1,0},{2,3},{3,2},{4,5},{5,4},{6,7},{7,6},{8,9},{9,8},{10,11... | collective-permute-start | bytes 2654216 | tf_op jit(solution)/shard_map/ppermute | solution.py:781
  1.2 23.1 %collective-permute-start.1 = (bf16[6,192,768]{2,1,0:T(8,128)(2,1)}, bf16[6,192,768]{2,1,0:T(8,128)(2,1)}, u32[]{:S(2)}, u32[]{:S(2)}) collective-permute-start(bf16[6,192,768]{2,1,0:T(8,128)(2,1)} %refs_1_.7), channel_id=1, source_target_pairs={{0,1},{1,0},{2,3},{3,2},{4,5},{5,4},{6,7},{7,6},{8,9},{9,8},{10,11... | collective-permute-start | bytes 5308424 | tf_op jit(solution)/shard_map/ppermute | solution.py:781
  19.1 22.5 %collective-permute-start.4 = (bf16[3,192,384]{2,1,0:T(8,128)(2,1)}, bf16[3,192,384]{2,1,0:T(8,128)(2,1)}, u32[]{:S(2)}, u32[]{:S(2)}) collective-permute-start(bf16[3,192,384]{2,1,0:T(8,128)(2,1)} %pad_maximum_fusion.4), channel_id=1, source_target_pairs={{0,2},{1,3},{2,0},{3,1},{4,6},{5,7},{6,4},{7,5},{8,10},{9,11},{10,... | collective-permute-start | bytes 1327112 | tf_op jit(solution)/shard_map/ppermute | solution.py:781
  44.8 32.8 %collective-permute-start.9 = (bf16[2,768,768]{2,1,0:T(8,128)(2,1)}, bf16[2,768,768]{2,1,0:T(8,128)(2,1)S(1)}, u32[]{:S(2)}, u32[]{:S(2)}) collective-permute-start(bf16[2,768,768]{2,1,0:T(8,128)(2,1)} %fi.5), channel_id=1, source_target_pairs={{0,1},{1,0},{2,3},{3,2},{4,5},{5,4},{6,7},{7,6},{8,9},{9,8},{10,11... | collective-permute-start | bytes 7077896 | tf_op jit(solution)/shard_map/ppermute | solution.py:781
  44.8 32.8 %collective-permute-start.10 = (bf16[2,768,768]{2,1,0:T(8,128)(2,1)}, bf16[2,768,768]{2,1,0:T(8,128)(2,1)S(1)}, u32[]{:S(2)}, u32[]{:S(2)}) collective-permute-start(bf16[2,768,768]{2,1,0:T(8,128)(2,1)} %fo.5), channel_id=1, source_target_pairs={{0,1},{1,0},{2,3},{3,2},{4,5},{5,4},{6,7},{7,6},{8,9},{9,8},{10,11... | collective-permute-start | bytes 7077896 | tf_op jit(solution)/shard_map/ppermute | solution.py:781
  51.3 26.3 %collective-permute-start.6 = (bf16[3,192,768]{2,1,0:T(8,128)(2,1)}, bf16[3,192,768]{2,1,0:T(8,128)(2,1)S(1)}, u32[]{:S(2)}, u32[]{:S(2)}) collective-permute-start(bf16[3,192,768]{2,1,0:T(8,128)(2,1)} %refs_2_.7), channel_id=1, source_target_pairs={{0,1},{1,0},{2,3},{3,2},{4,5},{5,4},{6,7},{7,6},{8,9},{9,8},{10,11... | collective-permute-start | bytes 2654216 | tf_op jit(solution)/shard_map/ppermute | solution.py:781
  132.4 22.2 %collective-permute-start.24 = (bf16[768,768]{1,0:T(8,128)(2,1)}, bf16[768,768]{1,0:T(8,128)(2,1)S(1)}, u32[]{:S(2)}, u32[]{:S(2)}) collective-permute-start(bf16[768,768]{1,0:T(8,128)(2,1)} %copy-done.66), channel_id=1, source_target_pairs={{0,1},{1,0},{2,3},{3,2},{4,5},{5,4},{6,7},{7,6},{8,9},{9,8},{10,11... | collective-permute-start | bytes 3538952 | tf_op jit(solution)/shard_map/ppermute | solution.py:781
  137.7 33.6 %collective-permute-start.26 = (bf16[384,768]{1,0:T(8,128)(2,1)}, bf16[384,768]{1,0:T(8,128)(2,1)}, u32[]{:S(2)}, u32[]{:S(2)}) collective-permute-start(bf16[384,768]{1,0:T(8,128)(2,1)} %add_convert_fusion.34), channel_id=1, source_target_pairs={{0,4},{4,0},{8,12},{12,8},{16,20},{20,16},{24,28},{28,24},{1,5},{5... | collective-permute-start | bytes 1769480 | tf_op jit(solution)/shard_map/ppermute | solution.py:861
  167.3 25.5 %collective-permute-start.28 = (bf16[4,192,768]{2,1,0:T(8,128)(2,1)}, bf16[4,192,768]{2,1,0:T(8,128)(2,1)}, u32[]{:S(2)}, u32[]{:S(2)}) collective-permute-start(bf16[4,192,768]{2,1,0:T(8,128)(2,1)} %get-tuple-element.233), channel_id=1, source_target_pairs={{0,1},{1,0},{2,3},{3,2},{4,5},{5,4},{6,7},{7,6},{8,9},{9,8},{10,11... | collective-permute-start | bytes 3538952 | tf_op jit(solution)/shard_map/ppermute | solution.py:781
  170.6 24.8 %collective-permute-start.25 = (bf16[512,768]{1,0:T(8,128)(2,1)}, bf16[512,768]{1,0:T(8,128)(2,1)}, u32[]{:S(2)}, u32[]{:S(2)}) collective-permute-start(bf16[512,768]{1,0:T(8,128)(2,1)} %copy-done.69), channel_id=1, source_target_pairs={{0,2},{1,3},{2,0},{3,1},{4,6},{5,7},{6,4},{7,5},{8,10},{9,11},{10,... | collective-permute-start | bytes 2359304 | tf_op jit(solution)/shard_map/ppermute | solution.py:781
  175.0 28.6 %collective-permute-start.30 = (bf16[384,768]{1,0:T(8,128)(2,1)}, bf16[384,768]{1,0:T(8,128)(2,1)}, u32[]{:S(2)}, u32[]{:S(2)}) collective-permute-start(bf16[384,768]{1,0:T(8,128)(2,1)} %get-tuple-element.220), channel_id=1, source_target_pairs={{0,8},{4,12},{24,16},{28,20},{1,9},{5,13},{25,17},{29,21},{2,10},{... | collective-permute-start | bytes 1769480 | tf_op jit(solution)/shard_map/ppermute | solution.py:861
  187.0 20.8 %collective-permute-start.29 = (bf16[4,192,768]{2,1,0:T(8,128)(2,1)}, bf16[4,192,768]{2,1,0:T(8,128)(2,1)}, u32[]{:S(2)}, u32[]{:S(2)}) collective-permute-start(bf16[4,192,768]{2,1,0:T(8,128)(2,1)} %get-tuple-element.239), channel_id=1, source_target_pairs={{0,1},{1,0},{2,3},{3,2},{4,5},{5,4},{6,7},{7,6},{8,9},{9,8},{10,11... | collective-permute-start | bytes 3538952 | tf_op jit(solution)/shard_map/ppermute | solution.py:781
  194.1 28.3 %collective-permute-start.32 = (bf16[384,768]{1,0:T(8,128)(2,1)S(1)}, bf16[384,768]{1,0:T(8,128)(2,1)S(1)}, u32[]{:S(2)}, u32[]{:S(2)}) collective-permute-start(bf16[384,768]{1,0:T(8,128)(2,1)S(1)} %add_convert_fusion.28), channel_id=1, source_target_pairs={{0,4},{4,0},{8,12},{12,8},{16,20},{20,16},{24,28},{28,24},{1,5},{5... | collective-permute-start | bytes 1769480 | tf_op jit(solution)/shard_map/ppermute | solution.py:861
  205.5 25.9 %collective-permute-start.31 = (bf16[768,768]{1,0:T(8,128)(2,1)S(1)}, bf16[768,768]{1,0:T(8,128)(2,1)S(1)}, u32[]{:S(2)}, u32[]{:S(2)}) collective-permute-start(bf16[768,768]{1,0:T(8,128)(2,1)S(1)} %get-tuple-element.248), channel_id=1, source_target_pairs={{0,1},{1,0},{2,3},{3,2},{4,5},{5,4},{6,7},{7,6},{8,9},{9,8},{10,11... | collective-permute-start | bytes 3538952 | tf_op jit(solution)/shard_map/ppermute | solution.py:781
  205.6 24.0 %collective-permute-start.37 = (bf16[384,768]{1,0:T(8,128)(2,1)S(1)}, bf16[384,768]{1,0:T(8,128)(2,1)S(1)}, u32[]{:S(2)}, u32[]{:S(2)}) collective-permute-start(bf16[384,768]{1,0:T(8,128)(2,1)S(1)} %add_convert_fusion.26), channel_id=1, source_target_pairs={{8,16},{12,20},{16,8},{20,12},{9,17},{13,21},{17,9},{21,13},{10,18... | collective-permute-start | bytes 1769480 | tf_op jit(solution)/shard_map/ppermute | solution.py:861
  206.4 37.4 %collective-permute-start.41 = (bf16[768,768]{1,0:T(8,128)(2,1)S(1)}, bf16[768,768]{1,0:T(8,128)(2,1)S(1)}, u32[]{:S(2)}, u32[]{:S(2)}) collective-permute-start(bf16[768,768]{1,0:T(8,128)(2,1)S(1)} %get-tuple-element.261), channel_id=1, source_target_pairs={{0,1},{1,0},{2,3},{3,2},{4,5},{5,4},{6,7},{7,6},{8,9},{9,8},{10,11... | collective-permute-start | bytes 3538952 | tf_op jit(solution)/shard_map/ppermute | solution.py:781
  210.0 42.0 %collective-permute-start.42 = (bf16[384,768]{1,0:T(8,128)(2,1)}, bf16[384,768]{1,0:T(8,128)(2,1)}, u32[]{:S(2)}, u32[]{:S(2)}) collective-permute-start(bf16[384,768]{1,0:T(8,128)(2,1)} %add_convert_fusion.27), channel_id=1, source_target_pairs={{0,4},{4,0},{8,12},{12,8},{16,20},{20,16},{24,28},{28,24},{1,5},{5... | collective-permute-start | bytes 1769480 | tf_op jit(solution)/shard_map/ppermute | solution.py:861
  224.6 22.6 %collective-permute-start.36 = (bf16[384,768]{1,0:T(8,128)(2,1)}, bf16[384,768]{1,0:T(8,128)(2,1)}, u32[]{:S(2)}, u32[]{:S(2)}) collective-permute-start(bf16[384,768]{1,0:T(8,128)(2,1)} %add_convert_fusion.22), channel_id=1, source_target_pairs={{0,8},{4,12},{24,16},{28,20},{1,9},{5,13},{25,17},{29,21},{2,10},{... | collective-permute-start | bytes 1769480 | tf_op jit(solution)/shard_map/ppermute | solution.py:861
  229.8 20.9 %collective-permute-start.39 = (bf16[384,768]{1,0:T(8,128)(2,1)S(1)}, bf16[384,768]{1,0:T(8,128)(2,1)}, u32[]{:S(2)}, u32[]{:S(2)}) collective-permute-start(bf16[384,768]{1,0:T(8,128)(2,1)S(1)} %add_convert_fusion.19), channel_id=1, source_target_pairs={{8,0},{12,4},{16,24},{20,28},{9,1},{13,5},{17,25},{21,29},{10,2},{... | collective-permute-start | bytes 1769480 | tf_op jit(solution)/shard_map/ppermute | solution.py:861
  243.8 20.4 %collective-permute-start.53 = (bf16[384,768]{1,0:T(8,128)(2,1)}, bf16[384,768]{1,0:T(8,128)(2,1)}, u32[]{:S(2)}, u32[]{:S(2)}) collective-permute-start(bf16[384,768]{1,0:T(8,128)(2,1)} %add_convert_fusion.25), channel_id=1, source_target_pairs={{0,4},{4,0},{8,12},{12,8},{16,20},{20,16},{24,28},{28,24},{1,5},{5... | collective-permute-start | bytes 1769480 | tf_op jit(solution)/shard_map/ppermute | solution.py:861
  250.7 32.3 %collective-permute-start.51 = (bf16[4,192,768]{2,1,0:T(8,128)(2,1)S(1)}, bf16[4,192,768]{2,1,0:T(8,128)(2,1)S(1)}, u32[]{:S(2)}, u32[]{:S(2)}) collective-permute-start(bf16[4,192,768]{2,1,0:T(8,128)(2,1)S(1)} %copy-done.68), channel_id=1, source_target_pairs={{0,1},{1,0},{2,3},{3,2},{4,5},{5,4},{6,7},{7,6},{8,9},{9,8},{10,11... | collective-permute-start | bytes 3538952 | tf_op jit(solution)/shard_map/ppermute | solution.py:781
  254.4 22.1 %collective-permute-start.43 = (bf16[384,768]{1,0:T(8,128)(2,1)S(1)}, bf16[384,768]{1,0:T(8,128)(2,1)S(1)}, u32[]{:S(2)}, u32[]{:S(2)}) collective-permute-start(bf16[384,768]{1,0:T(8,128)(2,1)S(1)} %copy-done.145), channel_id=1, source_target_pairs={{0,4},{4,0},{8,12},{12,8},{16,20},{20,16},{24,28},{28,24},{1,5},{5... | collective-permute-start | bytes 1769480 | tf_op jit(solution)/shard_map/ppermute | solution.py:861
  255.3 22.4 %collective-permute-start.46 = (bf16[384,768]{1,0:T(8,128)(2,1)S(1)}, bf16[384,768]{1,0:T(8,128)(2,1)S(1)}, u32[]{:S(2)}, u32[]{:S(2)}) collective-permute-start(bf16[384,768]{1,0:T(8,128)(2,1)S(1)} %add_convert_fusion.16), channel_id=1, source_target_pairs={{0,8},{4,12},{24,16},{28,20},{1,9},{5,13},{25,17},{29,21},{2,10},{... | collective-permute-start | bytes 1769480 | tf_op jit(solution)/shard_map/ppermute | solution.py:861
  266.8 23.1 %collective-permute-start.57 = (bf16[384,768]{1,0:T(8,128)(2,1)S(1)}, bf16[384,768]{1,0:T(8,128)(2,1)S(1)}, u32[]{:S(2)}, u32[]{:S(2)}) collective-permute-start(bf16[384,768]{1,0:T(8,128)(2,1)S(1)} %add_convert_fusion.9), channel_id=1, source_target_pairs={{0,8},{4,12},{24,16},{28,20},{1,9},{5,13},{25,17},{29,21},{2,10},{... | collective-permute-start | bytes 1769480 | tf_op jit(solution)/shard_map/ppermute | solution.py:861
  290.0 34.8 %collective-permute-start.54 = (bf16[400,768]{1,0:T(8,128)(2,1)S(1)}, bf16[400,768]{1,0:T(8,128)(2,1)S(1)}, u32[]{:S(2)}, u32[]{:S(2)}) collective-permute-start(bf16[400,768]{1,0:T(8,128)(2,1)S(1)} %pad_maximum_fusion.3), channel_id=1, source_target_pairs={{0,4},{4,0},{8,12},{12,8},{16,20},{20,16},{24,28},{28,24},{1,5},{5... | collective-permute-start | bytes 1843208 | tf_op jit(solution)/shard_map/ppermute | solution.py:861
  294.5 35.0 %collective-permute-start.45 = (bf16[384,768]{1,0:T(8,128)(2,1)S(1)}, bf16[384,768]{1,0:T(8,128)(2,1)S(1)}, u32[]{:S(2)}, u32[]{:S(2)}) collective-permute-start(bf16[384,768]{1,0:T(8,128)(2,1)S(1)} %broadcast_select_fusion.6), channel_id=1, source_target_pairs={{0,4},{4,0},{8,12},{12,8},{16,20},{20,16},{24,28},{28,24},{1,5},{5... | collective-permute-start | bytes 1769480 | tf_op jit(solution)/shard_map/ppermute | solution.py:861
  302.5 21.0 %collective-permute-start.50 = (bf16[384,768]{1,0:T(8,128)(2,1)S(1)}, bf16[384,768]{1,0:T(8,128)(2,1)S(1)}, u32[]{:S(2)}, u32[]{:S(2)}) collective-permute-start(bf16[384,768]{1,0:T(8,128)(2,1)S(1)} %add_convert_fusion.14), channel_id=1, source_target_pairs={{8,0},{12,4},{16,24},{20,28},{9,1},{13,5},{17,25},{21,29},{10,2},{... | collective-permute-start | bytes 1769480 | tf_op jit(solution)/shard_map/ppermute | solution.py:861
  304.4 31.7 %collective-permute-start.61 = (bf16[384,768]{1,0:T(8,128)(2,1)S(1)}, bf16[384,768]{1,0:T(8,128)(2,1)S(1)}, u32[]{:S(2)}, u32[]{:S(2)}) collective-permute-start(bf16[384,768]{1,0:T(8,128)(2,1)S(1)} %add_convert_fusion.7), channel_id=1, source_target_pairs={{8,0},{12,4},{16,24},{20,28},{9,1},{13,5},{17,25},{21,29},{10,2},{... | collective-permute-start | bytes 1769480 | tf_op jit(solution)/shard_map/ppermute | solution.py:861
  323.4 23.2 %collective-permute-start.67 = (bf16[384,768]{1,0:T(8,128)(2,1)S(1)}, bf16[384,768]{1,0:T(8,128)(2,1)S(1)}, u32[]{:S(2)}, u32[]{:S(2)}) collective-permute-start(bf16[384,768]{1,0:T(8,128)(2,1)S(1)} %add_convert_fusion.3), channel_id=1, source_target_pairs={{8,0},{12,4},{16,24},{20,28},{9,1},{13,5},{17,25},{21,29},{10,2},{... | collective-permute-start | bytes 1769480 | tf_op jit(solution)/shard_map/ppermute | solution.py:861
  336.1 22.7 %collective-permute-start.63 = (bf16[384,768]{1,0:T(8,128)(2,1)S(1)}, bf16[384,768]{1,0:T(8,128)(2,1)S(1)}, u32[]{:S(2)}, u32[]{:S(2)}) collective-permute-start(bf16[384,768]{1,0:T(8,128)(2,1)S(1)} %broadcast_select_fusion.2), channel_id=1, source_target_pairs={{0,4},{4,0},{8,12},{12,8},{16,20},{20,16},{24,28},{28,24},{1,5},{5... | collective-permute-start | bytes 1769480 | tf_op jit(solution)/shard_map/ppermute | solution.py:861
  338.8 20.5 %collective-permute-start.60 = (bf16[400,768]{1,0:T(8,128)(2,1)S(1)}, bf16[400,768]{1,0:T(8,128)(2,1)S(1)}, u32[]{:S(2)}, u32[]{:S(2)}) collective-permute-start(bf16[400,768]{1,0:T(8,128)(2,1)S(1)} %add_convert_fusion.1), channel_id=1, source_target_pairs={{8,16},{12,20},{16,8},{20,12},{9,17},{13,21},{17,9},{21,13},{10,18... | collective-permute-start | bytes 1843208 | tf_op jit(solution)/shard_map/ppermute | solution.py:861
  346.8 21.5 %collective-permute-start.56 = (bf16[384,768]{1,0:T(8,128)(2,1)S(1)}, bf16[384,768]{1,0:T(8,128)(2,1)S(1)}, u32[]{:S(2)}, u32[]{:S(2)}) collective-permute-start(bf16[384,768]{1,0:T(8,128)(2,1)S(1)} %broadcast_select_fusion.4), channel_id=1, source_target_pairs={{0,4},{4,0},{8,12},{12,8},{16,20},{20,16},{24,28},{28,24},{1,5},{5... | collective-permute-start | bytes 1769480 | tf_op jit(solution)/shard_map/ppermute | solution.py:861
  (188 other events, 1455.0 us)

commit v2 on v1

--- a/solution.py
+++ b/solution.py
@@ -129,7 +129,7 @@
         ),
         out_shape=tuple(kind for kind, _ in outs),
         input_output_aliases=aliases or {},
-        compiler_params=pltpu.CompilerParams(vmem_limit_bytes=25 << 20),
+        compiler_params=pltpu.CompilerParams(vmem_limit_bytes=20 << 20),
         cost_estimate=pl.CostEstimate(flops=flops, bytes_accessed=1 << 20, transcendentals=0),
     )(scalars, *[array for array, _ in ins])
 
@@ -1043,17 +1043,17 @@
     u_enc, u_self, u_cross = (
         u.reshape(4, quarter, D).astype(f32) for u in (unit_enc, unit_self, unit_cross)
     )
-    def placed(count, parts):
-        whole_grad = jnp.zeros((count, quarter, D), f32)
+    def placed(count, parts, rows=quarter):
+        whole_grad = jnp.zeros((count, rows, D), f32)
         for at, part in parts:
-            whole_grad = lax.dynamic_update_slice_in_dim(whole_grad, part, at, 0)
+            whole_grad = lax.dynamic_update_slice_in_dim(whole_grad, part.astype(f32), at, 0)
         return whole_grad
 
     query_grad = placed(3, ((2, u_cross[0:1]), (1, u_self[0:1]), (0, u_enc[0:1])))
     keyval_grad = placed(6, ((4, u_cross[1:3]), (2, u_self[1:3]), (0, u_enc[1:3])))
     output_grad = placed(3, ((2, u_cross[3:4]), (1, u_self[3:4]), (0, u_enc[3:4])))
-    feed_in_grad = jnp.stack([unit_in1, unit_in2]).astype(f32)
-    feed_out_grad = jnp.stack([unit_out1, unit_out2]).astype(f32)
+    feed_in_grad = placed(2, ((1, unit_in2[None]), (0, unit_in1[None])), hidden)
+    feed_out_grad = placed(2, ((1, unit_out2[None]), (0, unit_out1[None])), hidden)
     return (
         decoder_out, encoder_in_grad, decoder_in_grad, query_grad, keyval_grad, output_grad,
         feed_in_grad, feed_out_grad, gains, tables,

time: 401 us -> 401 us (level)
    dynamic_update_slice x0 -> x2, other arithmetic: none -> 4.99 us  [placed(): lax.dynamic_update_slice_in_dim(whole_grad, part.astype(f32), at, 0)]
    convert_element_type x2 -> x0, other arithmetic: 4.99 us -> none  [the longest x1 2.49 us: shards(): feed_out_grad = jnp.stack([unit_out1, unit_out2]).astype(f32)]
where the time goes in v2:
time: 401 us; the launch traced here: 397 us
  waiting for transfers between devices  103 us (26%)
  Pallas kernels  92.6 us (23%)
  starting transfers between devices  85.7 us (21%)
  local copies, waits for them, and re-layouts  56.3 us (14%)
  other arithmetic  49.5 us (12%)
  between operations  7.68 us (2%)
    pallas_call x13, Pallas kernels, call(): pl.pallas_call(kernel, grid_spec=pltpu.PrefetchScalarGridSpec(num_scalar_...  92.6 us
    ppermute x35, waiting for transfers between devices, step(): got = lax.ppermute(sent, 'dp', ROUTES[link])  72 us
    ppermute x35, starting transfers between devices, step(): got = lax.ppermute(sent, 'dp', ROUTES[link])  66.7 us
    unnamed x307, local copies, waits for them, and re-layouts  41.6 us
    convert_element_type x27, other arithmetic, add_low(): return (a.astype(f32) + b.astype(f32)).astype(bf16)  25.2 us
    ppermute x30, waiting for transfers between devices, swap_section(): return lax.ppermute(value, 'section', [(i, i ^ bit) for i in range(count)])  23.1 us
    ppermute x30, starting transfers between devices, swap_section(): return lax.ppermute(value, 'section', [(i, i ^ bit) for i in range(count)])  14.2 us
  transfers between devices with their start and end apart: 69, of which 22 were waited for; matrix products, arithmetic and copies ran while one was open for 16% of the time, Pallas kernels for 20%

profile of v2, /device:TPU:0, one launch (start us, length us, event | category | flops | bytes accessed | tf_op | source)
XLA Modules:
  0.0 396.6 jit_solution(14039282937314361119)
XLA Ops:
  4.7 3.0 collective-permute-start.2
  7.8 2.8 multiply_reduce_fusion
  26.1 8.7 %shard_map.240 = (bf16[3,512,384]{2,1,0:T(8,128)(2,1)S(1)}, bf16[512,384]{1,0:T(8,128)(2,1)S(1)}, bf16[6,384,384]{2,1,0:T(8,128)(2,1)S(1)}, bf16[6,128,128]{2,1,...) custom-call(s32[18]{0:T(128)S(1)} %concatenate.155.at, ...), custom_call_target="tpu_custom_call" | custom-call | flops 20000000000 | bytes 1048576 | tf_op jit(solution)/shard_map/pallas_call | solution.py:121
  46.4 4.8 %collective-permute-done.7.go = bf16[192,768]{1,0:T(8,128)(2,1)} collective-permute-done((bf16[192,768]{1,0:T(8,128)(2,1)}, bf16[192,768]{1,0:T(8,128)(2,1)}, u32[]{:S(2)}, u32[]{:S(2)}) %collective-permute-start.7) | collective-permute-done | bytes 294944 | tf_op jit(solution)/shard_map/ppermute | solution.py:781
  54.9 8.6 %shard_map.241 = (bf16[3,512,384]{2,1,0:T(8,128)(2,1)S(1)}, bf16[512,384]{1,0:T(8,128)(2,1)S(1)}, bf16[6,384,384]{2,1,0:T(8,128)(2,1)S(1)}, bf16[6,128,128]{2,1,0:T(8,128)(2,1)S(1)}, bf16[3,768,384]{2,1,0:T(8,128)(2,1)S(1)}) custom-call(s32[18]{0:T(128)S(1)} %concatenate.155.at, bf16[512,768]{1,0:T(8,128)(2,1)S(1)} %copy-done.115, f32[5,768]{1,0:T(8,128)S(1)} %copy-done.44, ...), custom_call_target="tpu_custom_call" | custom-call | flops 20000000000 | bytes 1048576 | tf_op jit(solution)/shard_map/pallas_call | solution.py:121
  68.7 6.0 %collective-permute-done.15 = bf16[4,48,768]{2,1,0:T(8,128)(2,1)S(1)} collective-permute-done((bf16[4,48,768]{2,1,0:T(8,128)(2,1)}, bf16[4,48,768]{2,1,0:T(8,128)(2,1)S(1)}, u32[]{:S(2)}, u32[]{:S(2)}) %collective-permute-start.15) | collective-permute-done | bytes 294944 | tf_op jit(solution)/shard_map/ppermute | solution.py:786
  78.1 9.4 %shard_map.242 = (bf16[512,768]{1,0:T(8,128)(2,1)S(1)}, bf16[512,768]{1,0:T(8,128)(2,1)S(1)}, bf16[512,1536]{1,0:T(8,128)(2,1)S(1)}, bf16[512,1536]{1,0:T(8,128)...) custom-call(s32[18]{0:T(128)S(1)} %concatenate.155.at, bf16[512,768]{1,0:T(8,128)(2,1)S(1)} %copy-done.112, ...), custom_call_target="tpu_custom_call" | custom-call | flops 20000000000 | bytes 1048576 | tf_op jit(solution)/shard_map/pallas_call | solution.py:121
  92.8 4.2 %shard_map.243 = (bf16[96,768]{1,0:T(8,128)(2,1)S(1)}, bf16[96,768]{1,0:T(8,128)(2,1)S(1)}, bf16[96,768]{1,0:T(8,128)(2,1)S(1)}, bf16[96,768]{1,0:T(8,128)(2,1)S...) custom-call(s32[18]{0:T(128)S(1)} %concatenate.155.at, ...), custom_call_target="tpu_custom_call" | custom-call | flops 100000000 | bytes 1048576 | tf_op jit(solution)/shard_map/pallas_call | solution.py:121
  101.0 10.2 %collective-permute-done.11.p1 = bf16[512,768]{1,0:T(8,128)(2,1)S(1)} collective-permute-done((bf16[512,768]{1,0:T(8,128)(2,1)S(1)}, bf16[512,768]{1,0:T(8,128)(2,1)S(1)}, u32[]{:S(2)}, u32[]{:S(2)}) %collective-permute-start.11) | collective-permute-done | bytes 786464 | tf_op jit(solution)/shard_map/ppermute | solution.py:781
  111.3 9.6 %shard_map.244 = (bf16[512,768]{1,0:T(8,128)(2,1)S(1)}, bf16[96,768]{1,0:T(8,128)(2,1)S(1)}, bf16[512,768]{1,0:T(8,128)(2,1)S(1)}, bf16[512,768]{1,0:T(8,128)(2,...) custom-call(s32[18]{0:T(128)S(1)} %concatenate.155.at, ...), custom_call_target="tpu_custom_call" | custom-call | flops 20000000000 | bytes 1048576 | tf_op jit(solution)/shard_map/pallas_call | solution.py:121
  121.0 3.7 shard_map.245
  147.8 6.8 %shard_map.246 = (bf16[96,768]{1,0:T(8,128)(2,1)S(1)}, bf16[96,768]{1,0:T(8,128)(2,1)S(1)}, bf16[512,768]{1,0:T(8,128)(2,1)S(1)}, bf16[512,768]{1,0:T(8,128)(2,1...) custom-call(s32[18]{0:T(128)S(1)} %concatenate.155.at, ...), custom_call_target="tpu_custom_call" | custom-call | flops 20000000000 | bytes 1048576 | tf_op jit(solution)/shard_map/pallas_call | solution.py:121
  157.3 6.3 %shard_map.247 = (bf16[512,1536]{1,0:T(8,128)(2,1)S(1)}, bf16[512,768]{1,0:T(8,128)(2,1)S(1)}) custom-call(s32[18]{0:T(128)S(1)} %concatenate.155.at, bf16[512,768]{1,0:T(8,128)(2,1)S(1)} %get-tuple-element.206.de_ref.refs_1_.refs_3_, bf16[512,1536]{1,0:T(8,128)(2,1)S(1)} %copy-done.98, bf16[2,768,768]{2,1,0:T(8,128)(2,1)S(1)} %copy-done.56, ...), custom_call_target="tpu_custom_call" | custom-call | flops 20000000000 | bytes 1048576 | tf_op jit(solution)/shard_map/pallas_call | solution.py:121
  171.3 3.8 add_convert_fusion.29
  175.0 3.2 collective-permute-start.30
  178.3 7.1 %shard_map.249 = (bf16[4,192,768]{2,1,0:T(8,128)(2,1)S(1)}, bf16[4,192,768]{2,1,0:T(8,128)(2,1)}, bf16[96,768]{1,0:T(8,128)(2,1)S(1)}, f32[1,768]{1,0:T(1,128)S(1)}, f32[3,32,128]{2,1,0:T(8,128)S(1)}) custom-call(s32[18]{0:T(128)S(1)} %concatenate.155.at, f32[96,768]{1,0:T(8,128)S(1)} %get-tuple-element.221.dm_ref, f32[5,768]{1,0:T(8,128)S(1)} %copy-done.46, ...), custom_call_target="tpu_custom_call" | custom-call | flops 1000000000 | bytes 1048576 | tf_op jit(solution)/shard_map/pallas_call | solution.py:121
  199.4 4.2 %shard_map.250 = (bf16[768,768]{1,0:T(8,128)(2,1)S(1)}, bf16[768,768]{1,0:T(8,128)(2,1)S(1)}, bf16[768,768]{1,0:T(8,128)(2,1)S(1)}, bf16[768,768]{1,0:T(8,128)(2,1)S(1)}) custom-call(s32[18]{0:T(128)S(1)} %concatenate.155.at, bf16[512,1536]{1,0:T(8,128)(2,1)S(1)} %copy-done.79, bf16[512,768]{1,0:T(8,128)(2,1)S(1)} %copy-done.85, ...), custom_call_target="tpu_custom_call" | custom-call | flops 10000000000 | bytes 1048576 | tf_op jit(solution)/shard_map/pallas_call | solution.py:121
  210.9 11.4 %shard_map.251 = (bf16[4,192,768]{2,1,0:T(8,128)(2,1)S(1)}, bf16[4,192,768]{2,1,0:T(8,128)(2,1)S(1)}, f32[6,3,512]{2,1,0:T(4,128)S(1)}, f32[6,1,256]{2,1,0:T(1,1...) custom-call(s32[18]{0:T(128)S(1)} %concatenate.155.at, ...), custom_call_target="tpu_custom_call" | custom-call | flops 20000000000 | bytes 1048576 | tf_op jit(solution)/shard_map/pallas_call | solution.py:121
  224.6 5.0 %collective-permute-start.36 = (bf16[384,768]{1,0:T(8,128)(2,1)}, bf16[384,768]{1,0:T(8,128)(2,1)}, u32[]{:S(2)}, u32[]{:S(2)}) collective-permute-start(bf16[384,768]{1,0:T(8,128)(2,1)} %add_convert_fusion.22), channel_id=1, source_target_pairs={{0,8},{4,12},{24,16},{28,20},{1,9},{5,13},{25,17},{29,21},{2,10},{... | collective-permute-start | bytes 1769480 | tf_op jit(solution)/shard_map/ppermute | solution.py:861
  234.0 9.8 %shard_map.252 = (bf16[4,192,768]{2,1,0:T(8,128)(2,1)S(1)}, bf16[4,192,768]{2,1,0:T(8,128)(2,1)S(1)}, f32[6,3,512]{2,1,0:T(4,128)S(1)}, f32[6,1,256]{2,1,0:T(1,1...) custom-call(s32[18]{0:T(128)S(1)} %concatenate.155.at, ...), custom_call_target="tpu_custom_call", output_to_operand_aliasing={{0}: (15, {}), {1}: (16, {})} | custom-call | flops 20000000000 | bytes 1048576 | tf_op jit(solution)/shard_map/pallas_call | solution.py:121
  255.4 8.0 %collective-permute-start.46 = (bf16[384,768]{1,0:T(8,128)(2,1)S(1)}, bf16[384,768]{1,0:T(8,128)(2,1)S(1)}, u32[]{:S(2)}, u32[]{:S(2)}) collective-permute-start(bf16[384,768]{1,0:T(8,128)(2,1)S(1)} %add_convert_fusion.16), channel_id=1, source_target_pairs={{0,8},{4,12},{24,16},{28,20},{1,9},{5,13},{25,17},{29,21},{2,10},{... | collective-permute-start | bytes 1769480 | tf_op jit(solution)/shard_map/ppermute | solution.py:861
  266.8 9.4 %collective-permute-start.57 = (bf16[384,768]{1,0:T(8,128)(2,1)S(1)}, bf16[384,768]{1,0:T(8,128)(2,1)S(1)}, u32[]{:S(2)}, u32[]{:S(2)}) collective-permute-start(bf16[384,768]{1,0:T(8,128)(2,1)S(1)} %add_convert_fusion.9), channel_id=1, source_target_pairs={{0,8},{4,12},{24,16},{28,20},{1,9},{5,13},{25,17},{29,21},{2,10},{... | collective-permute-start | bytes 1769480 | tf_op jit(solution)/shard_map/ppermute | solution.py:861
  279.1 2.8 collective-permute-done.49
  283.0 5.5 %collective-permute-start.65 = (bf16[384,768]{1,0:T(8,128)(2,1)S(1)}, bf16[384,768]{1,0:T(8,128)(2,1)S(1)}, u32[]{:S(2)}, u32[]{:S(2)}) collective-permute-start(bf16[384,768]{1,0:T(8,128)(2,1)S(1)} %add_convert_fusion.5), channel_id=1, source_target_pairs={{0,8},{4,12},{24,16},{28,20},{1,9},{5,13},{25,17},{29,21},{2,10},{... | collective-permute-start | bytes 1769480 | tf_op jit(solution)/shard_map/ppermute | solution.py:861
  295.5 5.9 %collective-permute-done.65 = bf16[384,768]{1,0:T(8,128)(2,1)S(1)} collective-permute-done((bf16[384,768]{1,0:T(8,128)(2,1)S(1)}, bf16[384,768]{1,0:T(8,128)(2,1)S(1)}, u32[]{:S(2)}, u32[]{:S(2)}) %collective-permute-start.65) | collective-permute-done | bytes 589856 | tf_op jit(solution)/shard_map/ppermute | solution.py:861
  305.9 17.6 %collective-permute-done.50 = bf16[384,768]{1,0:T(8,128)(2,1)S(1)} collective-permute-done((bf16[384,768]{1,0:T(8,128)(2,1)S(1)}, bf16[384,768]{1,0:T(8,128)(2,1)S(1)}, u32[]{:S(2)}, u32[]{:S(2)}) %collective-permute-start.50) | collective-permute-done | bytes 589856 | tf_op jit(solution)/shard_map/ppermute | solution.py:861
  324.9 4.6 %collective-permute-start.58 = (bf16[400,768]{1,0:T(8,128)(2,1)S(1)}, bf16[400,768]{1,0:T(8,128)(2,1)S(1)}, u32[]{:S(2)}, u32[]{:S(2)}) collective-permute-start(bf16[400,768]{1,0:T(8,128)(2,1)S(1)} %add_convert_fusion.2), channel_id=1, source_target_pairs={{0,8},{4,12},{24,16},{28,20},{1,9},{5,13},{25,17},{29,21},{2,10},{... | collective-permute-start | bytes 1843208 | tf_op jit(solution)/shard_map/ppermute | solution.py:861
  330.8 5.3 %collective-permute-done.61 = bf16[384,768]{1,0:T(8,128)(2,1)S(1)} collective-permute-done((bf16[384,768]{1,0:T(8,128)(2,1)S(1)}, bf16[384,768]{1,0:T(8,128)(2,1)S(1)}, u32[]{:S(2)}, u32[]{:S(2)}) %collective-permute-start.61) | collective-permute-done | bytes 589856 | tf_op jit(solution)/shard_map/ppermute | solution.py:861
  341.3 5.4 %collective-permute-done.67 = bf16[384,768]{1,0:T(8,128)(2,1)S(1)} collective-permute-done((bf16[384,768]{1,0:T(8,128)(2,1)S(1)}, bf16[384,768]{1,0:T(8,128)(2,1)S(1)}, u32[]{:S(2)}, u32[]{:S(2)}) %collective-permute-start.67) | collective-permute-done | bytes 589856 | tf_op jit(solution)/shard_map/ppermute | solution.py:861
  348.2 10.6 %collective-permute-done.63 = bf16[384,768]{1,0:T(8,128)(2,1)S(1)} collective-permute-done((bf16[384,768]{1,0:T(8,128)(2,1)S(1)}, bf16[384,768]{1,0:T(8,128)(2,1)S(1)}, u32[]{:S(2)}, u32[]{:S(2)}) %collective-permute-start.63) | collective-permute-done | bytes 589856 | tf_op jit(solution)/shard_map/ppermute | solution.py:861
  363.3 5.0 %collective-permute-done.56 = bf16[384,768]{1,0:T(8,128)(2,1)S(1)} collective-permute-done((bf16[384,768]{1,0:T(8,128)(2,1)S(1)}, bf16[384,768]{1,0:T(8,128)(2,1)S(1)}, u32[]{:S(2)}, u32[]{:S(2)}) %collective-permute-start.56) | collective-permute-done | bytes 589856 | tf_op jit(solution)/shard_map/ppermute | solution.py:861
  373.4 11.6 %collective-permute-done.68 = bf16[384,768]{1,0:T(8,128)(2,1)S(1)} collective-permute-done((bf16[384,768]{1,0:T(8,128)(2,1)S(1)}, bf16[384,768]{1,0:T(8,128)(2,1)S(1)}, u32[]{:S(2)}, u32[]{:S(2)}) %collective-permute-start.68) | collective-permute-done | bytes 589856 | tf_op jit(solution)/shard_map/ppermute | solution.py:861
  (530 shorter events, 168.6 us)
Async XLA Ops:
  0.7 23.6 %collective-permute-start = (bf16[3,192,768]{2,1,0:T(8,128)(2,1)}, bf16[3,192,768]{2,1,0:T(8,128)(2,1)S(1)}, u32[]{:S(2)}, u32[]{:S(2)}) collective-permute-start(bf16[3,192,768]{2,1,0:T(8,128)(2,1)} %refs_0_.7), channel_id=1, source_target_pairs={{0,1},{1,0},{2,3},{3,2},{4,5},{5,4},{6,7},{7,6},{8,9},{9,8},{10,11... | collective-permute-start | bytes 2654216 | tf_op jit(solution)/shard_map/ppermute | solution.py:781
  1.2 23.1 %collective-permute-start.1 = (bf16[6,192,768]{2,1,0:T(8,128)(2,1)}, bf16[6,192,768]{2,1,0:T(8,128)(2,1)}, u32[]{:S(2)}, u32[]{:S(2)}) collective-permute-start(bf16[6,192,768]{2,1,0:T(8,128)(2,1)} %refs_1_.7), channel_id=1, source_target_pairs={{0,1},{1,0},{2,3},{3,2},{4,5},{5,4},{6,7},{7,6},{8,9},{9,8},{10,11... | collective-permute-start | bytes 5308424 | tf_op jit(solution)/shard_map/ppermute | solution.py:781
  19.1 22.5 %collective-permute-start.4 = (bf16[3,192,384]{2,1,0:T(8,128)(2,1)}, bf16[3,192,384]{2,1,0:T(8,128)(2,1)}, u32[]{:S(2)}, u32[]{:S(2)}) collective-permute-start(bf16[3,192,384]{2,1,0:T(8,128)(2,1)} %pad_maximum_fusion.4), channel_id=1, source_target_pairs={{0,2},{1,3},{2,0},{3,1},{4,6},{5,7},{6,4},{7,5},{8,10},{9,11},{10,... | collective-permute-start | bytes 1327112 | tf_op jit(solution)/shard_map/ppermute | solution.py:781
  44.8 32.8 %collective-permute-start.9 = (bf16[2,768,768]{2,1,0:T(8,128)(2,1)}, bf16[2,768,768]{2,1,0:T(8,128)(2,1)S(1)}, u32[]{:S(2)}, u32[]{:S(2)}) collective-permute-start(bf16[2,768,768]{2,1,0:T(8,128)(2,1)} %fi.5), channel_id=1, source_target_pairs={{0,1},{1,0},{2,3},{3,2},{4,5},{5,4},{6,7},{7,6},{8,9},{9,8},{10,11... | collective-permute-start | bytes 7077896 | tf_op jit(solution)/shard_map/ppermute | solution.py:781
  44.8 32.8 %collective-permute-start.10 = (bf16[2,768,768]{2,1,0:T(8,128)(2,1)}, bf16[2,768,768]{2,1,0:T(8,128)(2,1)S(1)}, u32[]{:S(2)}, u32[]{:S(2)}) collective-permute-start(bf16[2,768,768]{2,1,0:T(8,128)(2,1)} %fo.5), channel_id=1, source_target_pairs={{0,1},{1,0},{2,3},{3,2},{4,5},{5,4},{6,7},{7,6},{8,9},{9,8},{10,11... | collective-permute-start | bytes 7077896 | tf_op jit(solution)/shard_map/ppermute | solution.py:781
  51.3 26.3 %collective-permute-start.6 = (bf16[3,192,768]{2,1,0:T(8,128)(2,1)}, bf16[3,192,768]{2,1,0:T(8,128)(2,1)S(1)}, u32[]{:S(2)}, u32[]{:S(2)}) collective-permute-start(bf16[3,192,768]{2,1,0:T(8,128)(2,1)} %refs_2_.7), channel_id=1, source_target_pairs={{0,1},{1,0},{2,3},{3,2},{4,5},{5,4},{6,7},{7,6},{8,9},{9,8},{10,11... | collective-permute-start | bytes 2654216 | tf_op jit(solution)/shard_map/ppermute | solution.py:781
  132.4 22.2 %collective-permute-start.24 = (bf16[768,768]{1,0:T(8,128)(2,1)}, bf16[768,768]{1,0:T(8,128)(2,1)S(1)}, u32[]{:S(2)}, u32[]{:S(2)}) collective-permute-start(bf16[768,768]{1,0:T(8,128)(2,1)} %copy-done.66), channel_id=1, source_target_pairs={{0,1},{1,0},{2,3},{3,2},{4,5},{5,4},{6,7},{7,6},{8,9},{9,8},{10,11... | collective-permute-start | bytes 3538952 | tf_op jit(solution)/shard_map/ppermute | solution.py:781
  137.7 33.6 %collective-permute-start.26 = (bf16[384,768]{1,0:T(8,128)(2,1)}, bf16[384,768]{1,0:T(8,128)(2,1)}, u32[]{:S(2)}, u32[]{:S(2)}) collective-permute-start(bf16[384,768]{1,0:T(8,128)(2,1)} %add_convert_fusion.34), channel_id=1, source_target_pairs={{0,4},{4,0},{8,12},{12,8},{16,20},{20,16},{24,28},{28,24},{1,5},{5... | collective-permute-start | bytes 1769480 | tf_op jit(solution)/shard_map/ppermute | solution.py:861
  167.4 25.5 %collective-permute-start.28 = (bf16[4,192,768]{2,1,0:T(8,128)(2,1)}, bf16[4,192,768]{2,1,0:T(8,128)(2,1)}, u32[]{:S(2)}, u32[]{:S(2)}) collective-permute-start(bf16[4,192,768]{2,1,0:T(8,128)(2,1)} %get-tuple-element.233), channel_id=1, source_target_pairs={{0,1},{1,0},{2,3},{3,2},{4,5},{5,4},{6,7},{7,6},{8,9},{9,8},{10,11... | collective-permute-start | bytes 3538952 | tf_op jit(solution)/shard_map/ppermute | solution.py:781
  170.6 24.8 %collective-permute-start.25 = (bf16[512,768]{1,0:T(8,128)(2,1)}, bf16[512,768]{1,0:T(8,128)(2,1)}, u32[]{:S(2)}, u32[]{:S(2)}) collective-permute-start(bf16[512,768]{1,0:T(8,128)(2,1)} %copy-done.69), channel_id=1, source_target_pairs={{0,2},{1,3},{2,0},{3,1},{4,6},{5,7},{6,4},{7,5},{8,10},{9,11},{10,... | collective-permute-start | bytes 2359304 | tf_op jit(solution)/shard_map/ppermute | solution.py:781
  175.0 28.6 %collective-permute-start.30 = (bf16[384,768]{1,0:T(8,128)(2,1)}, bf16[384,768]{1,0:T(8,128)(2,1)}, u32[]{:S(2)}, u32[]{:S(2)}) collective-permute-start(bf16[384,768]{1,0:T(8,128)(2,1)} %get-tuple-element.220), channel_id=1, source_target_pairs={{0,8},{4,12},{24,16},{28,20},{1,9},{5,13},{25,17},{29,21},{2,10},{... | collective-permute-start | bytes 1769480 | tf_op jit(solution)/shard_map/ppermute | solution.py:861
  187.0 20.8 %collective-permute-start.29 = (bf16[4,192,768]{2,1,0:T(8,128)(2,1)}, bf16[4,192,768]{2,1,0:T(8,128)(2,1)}, u32[]{:S(2)}, u32[]{:S(2)}) collective-permute-start(bf16[4,192,768]{2,1,0:T(8,128)(2,1)} %get-tuple-element.239), channel_id=1, source_target_pairs={{0,1},{1,0},{2,3},{3,2},{4,5},{5,4},{6,7},{7,6},{8,9},{9,8},{10,11... | collective-permute-start | bytes 3538952 | tf_op jit(solution)/shard_map/ppermute | solution.py:781
  194.1 28.3 %collective-permute-start.32 = (bf16[384,768]{1,0:T(8,128)(2,1)S(1)}, bf16[384,768]{1,0:T(8,128)(2,1)S(1)}, u32[]{:S(2)}, u32[]{:S(2)}) collective-permute-start(bf16[384,768]{1,0:T(8,128)(2,1)S(1)} %add_convert_fusion.28), channel_id=1, source_target_pairs={{0,4},{4,0},{8,12},{12,8},{16,20},{20,16},{24,28},{28,24},{1,5},{5... | collective-permute-start | bytes 1769480 | tf_op jit(solution)/shard_map/ppermute | solution.py:861
  205.5 25.9 %collective-permute-start.31 = (bf16[768,768]{1,0:T(8,128)(2,1)S(1)}, bf16[768,768]{1,0:T(8,128)(2,1)S(1)}, u32[]{:S(2)}, u32[]{:S(2)}) collective-permute-start(bf16[768,768]{1,0:T(8,128)(2,1)S(1)} %get-tuple-element.248), channel_id=1, source_target_pairs={{0,1},{1,0},{2,3},{3,2},{4,5},{5,4},{6,7},{7,6},{8,9},{9,8},{10,11... | collective-permute-start | bytes 3538952 | tf_op jit(solution)/shard_map/ppermute | solution.py:781
  205.6 24.0 %collective-permute-start.37 = (bf16[384,768]{1,0:T(8,128)(2,1)S(1)}, bf16[384,768]{1,0:T(8,128)(2,1)S(1)}, u32[]{:S(2)}, u32[]{:S(2)}) collective-permute-start(bf16[384,768]{1,0:T(8,128)(2,1)S(1)} %add_convert_fusion.26), channel_id=1, source_target_pairs={{8,16},{12,20},{16,8},{20,12},{9,17},{13,21},{17,9},{21,13},{10,18... | collective-permute-start | bytes 1769480 | tf_op jit(solution)/shard_map/ppermute | solution.py:861
  206.5 37.4 %collective-permute-start.41 = (bf16[768,768]{1,0:T(8,128)(2,1)S(1)}, bf16[768,768]{1,0:T(8,128)(2,1)S(1)}, u32[]{:S(2)}, u32[]{:S(2)}) collective-permute-start(bf16[768,768]{1,0:T(8,128)(2,1)S(1)} %get-tuple-element.261), channel_id=1, source_target_pairs={{0,1},{1,0},{2,3},{3,2},{4,5},{5,4},{6,7},{7,6},{8,9},{9,8},{10,11... | collective-permute-start | bytes 3538952 | tf_op jit(solution)/shard_map/ppermute | solution.py:781
  210.0 42.0 %collective-permute-start.42 = (bf16[384,768]{1,0:T(8,128)(2,1)}, bf16[384,768]{1,0:T(8,128)(2,1)}, u32[]{:S(2)}, u32[]{:S(2)}) collective-permute-start(bf16[384,768]{1,0:T(8,128)(2,1)} %add_convert_fusion.27), channel_id=1, source_target_pairs={{0,4},{4,0},{8,12},{12,8},{16,20},{20,16},{24,28},{28,24},{1,5},{5... | collective-permute-start | bytes 1769480 | tf_op jit(solution)/shard_map/ppermute | solution.py:861
  224.6 22.6 %collective-permute-start.36 = (bf16[384,768]{1,0:T(8,128)(2,1)}, bf16[384,768]{1,0:T(8,128)(2,1)}, u32[]{:S(2)}, u32[]{:S(2)}) collective-permute-start(bf16[384,768]{1,0:T(8,128)(2,1)} %add_convert_fusion.22), channel_id=1, source_target_pairs={{0,8},{4,12},{24,16},{28,20},{1,9},{5,13},{25,17},{29,21},{2,10},{... | collective-permute-start | bytes 1769480 | tf_op jit(solution)/shard_map/ppermute | solution.py:861
  229.8 20.9 %collective-permute-start.39 = (bf16[384,768]{1,0:T(8,128)(2,1)S(1)}, bf16[384,768]{1,0:T(8,128)(2,1)}, u32[]{:S(2)}, u32[]{:S(2)}) collective-permute-start(bf16[384,768]{1,0:T(8,128)(2,1)S(1)} %add_convert_fusion.19), channel_id=1, source_target_pairs={{8,0},{12,4},{16,24},{20,28},{9,1},{13,5},{17,25},{21,29},{10,2},{... | collective-permute-start | bytes 1769480 | tf_op jit(solution)/shard_map/ppermute | solution.py:861
  243.8 20.4 %collective-permute-start.53 = (bf16[384,768]{1,0:T(8,128)(2,1)}, bf16[384,768]{1,0:T(8,128)(2,1)}, u32[]{:S(2)}, u32[]{:S(2)}) collective-permute-start(bf16[384,768]{1,0:T(8,128)(2,1)} %add_convert_fusion.25), channel_id=1, source_target_pairs={{0,4},{4,0},{8,12},{12,8},{16,20},{20,16},{24,28},{28,24},{1,5},{5... | collective-permute-start | bytes 1769480 | tf_op jit(solution)/shard_map/ppermute | solution.py:861
  250.7 32.3 %collective-permute-start.51 = (bf16[4,192,768]{2,1,0:T(8,128)(2,1)S(1)}, bf16[4,192,768]{2,1,0:T(8,128)(2,1)S(1)}, u32[]{:S(2)}, u32[]{:S(2)}) collective-permute-start(bf16[4,192,768]{2,1,0:T(8,128)(2,1)S(1)} %copy-done.68), channel_id=1, source_target_pairs={{0,1},{1,0},{2,3},{3,2},{4,5},{5,4},{6,7},{7,6},{8,9},{9,8},{10,11... | collective-permute-start | bytes 3538952 | tf_op jit(solution)/shard_map/ppermute | solution.py:781
  254.4 22.1 %collective-permute-start.43 = (bf16[384,768]{1,0:T(8,128)(2,1)S(1)}, bf16[384,768]{1,0:T(8,128)(2,1)S(1)}, u32[]{:S(2)}, u32[]{:S(2)}) collective-permute-start(bf16[384,768]{1,0:T(8,128)(2,1)S(1)} %copy-done.145), channel_id=1, source_target_pairs={{0,4},{4,0},{8,12},{12,8},{16,20},{20,16},{24,28},{28,24},{1,5},{5... | collective-permute-start | bytes 1769480 | tf_op jit(solution)/shard_map/ppermute | solution.py:861
  255.4 22.4 %collective-permute-start.46 = (bf16[384,768]{1,0:T(8,128)(2,1)S(1)}, bf16[384,768]{1,0:T(8,128)(2,1)S(1)}, u32[]{:S(2)}, u32[]{:S(2)}) collective-permute-start(bf16[384,768]{1,0:T(8,128)(2,1)S(1)} %add_convert_fusion.16), channel_id=1, source_target_pairs={{0,8},{4,12},{24,16},{28,20},{1,9},{5,13},{25,17},{29,21},{2,10},{... | collective-permute-start | bytes 1769480 | tf_op jit(solution)/shard_map/ppermute | solution.py:861
  266.8 23.1 %collective-permute-start.57 = (bf16[384,768]{1,0:T(8,128)(2,1)S(1)}, bf16[384,768]{1,0:T(8,128)(2,1)S(1)}, u32[]{:S(2)}, u32[]{:S(2)}) collective-permute-start(bf16[384,768]{1,0:T(8,128)(2,1)S(1)} %add_convert_fusion.9), channel_id=1, source_target_pairs={{0,8},{4,12},{24,16},{28,20},{1,9},{5,13},{25,17},{29,21},{2,10},{... | collective-permute-start | bytes 1769480 | tf_op jit(solution)/shard_map/ppermute | solution.py:861
  290.0 34.8 %collective-permute-start.54 = (bf16[400,768]{1,0:T(8,128)(2,1)S(1)}, bf16[400,768]{1,0:T(8,128)(2,1)S(1)}, u32[]{:S(2)}, u32[]{:S(2)}) collective-permute-start(bf16[400,768]{1,0:T(8,128)(2,1)S(1)} %pad_maximum_fusion.3), channel_id=1, source_target_pairs={{0,4},{4,0},{8,12},{12,8},{16,20},{20,16},{24,28},{28,24},{1,5},{5... | collective-permute-start | bytes 1843208 | tf_op jit(solution)/shard_map/ppermute | solution.py:861
  294.6 35.0 %collective-permute-start.45 = (bf16[384,768]{1,0:T(8,128)(2,1)S(1)}, bf16[384,768]{1,0:T(8,128)(2,1)S(1)}, u32[]{:S(2)}, u32[]{:S(2)}) collective-permute-start(bf16[384,768]{1,0:T(8,128)(2,1)S(1)} %broadcast_select_fusion.6), channel_id=1, source_target_pairs={{0,4},{4,0},{8,12},{12,8},{16,20},{20,16},{24,28},{28,24},{1,5},{5... | collective-permute-start | bytes 1769480 | tf_op jit(solution)/shard_map/ppermute | solution.py:861
  302.5 21.0 %collective-permute-start.50 = (bf16[384,768]{1,0:T(8,128)(2,1)S(1)}, bf16[384,768]{1,0:T(8,128)(2,1)S(1)}, u32[]{:S(2)}, u32[]{:S(2)}) collective-permute-start(bf16[384,768]{1,0:T(8,128)(2,1)S(1)} %add_convert_fusion.14), channel_id=1, source_target_pairs={{8,0},{12,4},{16,24},{20,28},{9,1},{13,5},{17,25},{21,29},{10,2},{... | collective-permute-start | bytes 1769480 | tf_op jit(solution)/shard_map/ppermute | solution.py:861
  304.4 31.7 %collective-permute-start.61 = (bf16[384,768]{1,0:T(8,128)(2,1)S(1)}, bf16[384,768]{1,0:T(8,128)(2,1)S(1)}, u32[]{:S(2)}, u32[]{:S(2)}) collective-permute-start(bf16[384,768]{1,0:T(8,128)(2,1)S(1)} %add_convert_fusion.7), channel_id=1, source_target_pairs={{8,0},{12,4},{16,24},{20,28},{9,1},{13,5},{17,25},{21,29},{10,2},{... | collective-permute-start | bytes 1769480 | tf_op jit(solution)/shard_map/ppermute | solution.py:861
  323.5 23.2 %collective-permute-start.67 = (bf16[384,768]{1,0:T(8,128)(2,1)S(1)}, bf16[384,768]{1,0:T(8,128)(2,1)S(1)}, u32[]{:S(2)}, u32[]{:S(2)}) collective-permute-start(bf16[384,768]{1,0:T(8,128)(2,1)S(1)} %add_convert_fusion.3), channel_id=1, source_target_pairs={{8,0},{12,4},{16,24},{20,28},{9,1},{13,5},{17,25},{21,29},{10,2},{... | collective-permute-start | bytes 1769480 | tf_op jit(solution)/shard_map/ppermute | solution.py:861
  336.2 22.7 %collective-permute-start.63 = (bf16[384,768]{1,0:T(8,128)(2,1)S(1)}, bf16[384,768]{1,0:T(8,128)(2,1)S(1)}, u32[]{:S(2)}, u32[]{:S(2)}) collective-permute-start(bf16[384,768]{1,0:T(8,128)(2,1)S(1)} %broadcast_select_fusion.2), channel_id=1, source_target_pairs={{0,4},{4,0},{8,12},{12,8},{16,20},{20,16},{24,28},{28,24},{1,5},{5... | collective-permute-start | bytes 1769480 | tf_op jit(solution)/shard_map/ppermute | solution.py:861
  338.9 20.5 %collective-permute-start.60 = (bf16[400,768]{1,0:T(8,128)(2,1)S(1)}, bf16[400,768]{1,0:T(8,128)(2,1)S(1)}, u32[]{:S(2)}, u32[]{:S(2)}) collective-permute-start(bf16[400,768]{1,0:T(8,128)(2,1)S(1)} %add_convert_fusion.1), channel_id=1, source_target_pairs={{8,16},{12,20},{16,8},{20,12},{9,17},{13,21},{17,9},{21,13},{10,18... | collective-permute-start | bytes 1843208 | tf_op jit(solution)/shard_map/ppermute | solution.py:861
  346.8 21.5 %collective-permute-start.56 = (bf16[384,768]{1,0:T(8,128)(2,1)S(1)}, bf16[384,768]{1,0:T(8,128)(2,1)S(1)}, u32[]{:S(2)}, u32[]{:S(2)}) collective-permute-start(bf16[384,768]{1,0:T(8,128)(2,1)S(1)} %broadcast_select_fusion.4), channel_id=1, source_target_pairs={{0,4},{4,0},{8,12},{12,8},{16,20},{20,16},{24,28},{28,24},{1,5},{5... | collective-permute-start | bytes 1769480 | tf_op jit(solution)/shard_map/ppermute | solution.py:861
  (188 other events, 1455.0 us)
